TPU v7x, 256 devices: a whole 4x4x8 slice. The times are simulated.
256 devices in a mesh: dp: 32 (over x, z_lo, y), section: 8 (over z_hi, core).
Axes of the slice: x: 4, y: 4, z: 8 (z_hi: 4, z_lo: 2; z = z_hi * 2 + z_lo), core: 2. Of those that a mesh axis runs over, the one named last changes fastest.
Arguments:
- latents: bfloat16 [2, 2048, 1152], P(None, 'dp'), may hold values from -6 to 6
- time_table: bfloat16 [1000, 1152], replicated, may hold values from -3 to 3
- timesteps: int32 [2], replicated, may hold values from 0 to 999
- order: int32 [2], replicated, may hold values from 0 to 1, each once
- gains: bfloat16 [8, 1152], P('section'), may hold values from 0.099609375 to 1.8984375
- w_up: bfloat16 [8, 1152, 2304], P('section', 'dp'), may hold values from -0.1875 to 0.1875
- w_down: bfloat16 [8, 2304, 1152], P('section', 'dp'), may hold values from -0.125 to 0.125
- w_join: bfloat16 [8, 1152, 1152], P('section', 'dp'), may hold values from -0.125 to 0.125
- cotangent: bfloat16 [2, 2048, 1152], P(None, 'dp'), may hold values from -0.09375 to 0.09375
Outputs:
- grad_up: float32 [8, 1152, 2304], P('section', 'dp')
- grad_down: float32 [8, 2304, 1152], P('section', 'dp')
- grad_join: float32 [8, 1152, 1152], P('section', 'dp')
Inputs may be any that keep to these rules, and one draw needn't show every extreme that they name: order names each of the 2 micro-batches once.
All inputs are finite; a program needn't handle non-finite values.
Results may differ from a plain program's by a relative error of at most 0.04.
Values may be sent and summed in bfloat16 or wider, within the bound.
A program may use at most 128 MiB of HBM per device.

v0:
```python
import jax
import jax.numpy as jnp
from jax import lax
from jax.sharding import PartitionSpec as P

EPSILON = 1e-06


def from_partner(block, axis, apart):
    count = lax.axis_size(axis)
    route = []
    for low in range(count):
        high = low | 1 << apart
        if high != low and high < count:
            route += [(low, high), (high, low)]
    return lax.ppermute(block, axis, route)


def passed_along(x, axis, by):
    devices = lax.axis_size(axis)
    pairs = [(i, i + by) for i in range(devices) if 0 <= i + by < devices]
    return lax.ppermute(x, axis, pairs)


def gelu_tanh(values):
    return jax.nn.gelu(values, approximate=True)


def norm_parts(inputs, gain_row):
    values = inputs.astype(jnp.float32)
    center = values - jnp.mean(values, axis=-1, keepdims=True)
    inverse = lax.rsqrt(jnp.mean(center * center, axis=-1, keepdims=True) + EPSILON)
    normed = center * inverse
    scaled = (normed * gain_row.astype(jnp.float32)).astype(jnp.bfloat16)
    return (normed, inverse, scaled)


def block_forward(inputs, gain_row, up_full, down_full):
    normed, inverse, scaled = norm_parts(inputs, gain_row)
    preact = jnp.dot(scaled, up_full, preferred_element_type=jnp.float32)
    active = gelu_tanh(preact).astype(jnp.bfloat16)
    added = jnp.dot(active, down_full, preferred_element_type=jnp.float32)
    return (inputs.astype(jnp.float32) + added).astype(jnp.bfloat16)


def block_backward(inputs, gain_row, up_full, down_full, cotangent_in):
    normed, inverse, scaled = norm_parts(inputs, gain_row)
    preact = jnp.dot(scaled, up_full, preferred_element_type=jnp.float32)
    active = gelu_tanh(preact).astype(jnp.bfloat16)
    back_in = jnp.dot(cotangent_in, down_full.T, preferred_element_type=jnp.float32)
    unused, pullback = jax.vjp(gelu_tanh, preact)
    grad_pre = pullback(back_in)[0].astype(jnp.bfloat16)
    grad_scaled = jnp.dot(grad_pre, up_full.T, preferred_element_type=jnp.float32)
    grad_normed = grad_scaled * gain_row.astype(jnp.float32)
    first_mean = jnp.mean(grad_normed, axis=-1, keepdims=True)
    second_mean = jnp.mean(grad_normed * normed, axis=-1, keepdims=True)
    grad_mixture = (grad_normed - first_mean - normed * second_mean) * inverse
    grad_input = (cotangent_in.astype(jnp.float32) + grad_mixture).astype(jnp.bfloat16)
    return (grad_input, scaled, active, grad_pre)


def put_slot(buffer, slot_index, value, landing):
    current = lax.dynamic_index_in_dim(buffer, slot_index, 0, keepdims=False)
    return lax.dynamic_update_index_in_dim(
        buffer, jnp.where(landing, value, current), slot_index, 0
    )


def mirror_forward(values, sections):
    carried = values
    for bit_index in range(sections.bit_length() - 1):
        carried = from_partner(carried, "section", bit_index)
    return carried


def mirror_backward(values, sections):
    carried = values
    for bit_index in range(sections.bit_length() - 1):
        carried = from_partner(carried, "section", bit_index)
    return carried


def local(latents, time_table, timesteps, order, gains, w_up, w_down, w_join, cotangent):
    sections = lax.axis_size("section")
    halfway = sections // 2
    position = lax.axis_index("section")
    is_deep = position >= halfway
    micro_count, row_count, features = latents.shape
    gain_row = gains[0]
    up_full, down_full, join_full = (
        lax.all_gather(w_up, "dp", axis=1, tiled=True),
        lax.all_gather(w_down, "dp", axis=1, tiled=True),
        lax.all_gather(w_join, "dp", axis=1, tiled=True),
    )
    up_full = up_full[0]
    down_full = down_full[0]
    join_full = join_full[0]
    blank = jnp.zeros((row_count, features), jnp.bfloat16)
    blank_stack = jnp.zeros((micro_count, row_count, features), jnp.bfloat16)
    wide_stack = jnp.zeros((micro_count, row_count, up_full.shape[1]), jnp.bfloat16)

    def forward_tick(tick_index, carried_state, sending):
        incoming, skip_buffer, left_buffer, input_buffer = carried_state
        micro_index = tick_index - position
        active_tick = (micro_index >= 0) & (micro_index < micro_count)
        slot_index = jnp.clip(micro_index, 0, micro_count - 1)
        picked = order[slot_index]
        initial = (
            latents[picked].astype(jnp.float32)
            + time_table[timesteps[slot_index]].astype(jnp.float32)[None, :]
        )
        arriving = jnp.where(position == 0, initial.astype(jnp.bfloat16), incoming)
        skip_here = lax.dynamic_index_in_dim(skip_buffer, slot_index, 0, keepdims=False)

        def forward_compute(operands):
            stream_in, skip_in = operands
            joining = lax.cond(
                is_deep,
                lambda: (
                    jnp.dot(stream_in, join_full, preferred_element_type=jnp.float32)
                    + skip_in.astype(jnp.float32)
                ).astype(jnp.bfloat16),
                lambda: stream_in,
            )
            result = block_forward(joining, gain_row, up_full, down_full)
            skip_out = lax.cond(
                is_deep,
                lambda: jnp.zeros_like(result),
                lambda: jnp.dot(result, join_full, preferred_element_type=jnp.float32).astype(
                    jnp.bfloat16
                ),
            )
            left_side = jnp.where(is_deep, stream_in, result)
            return (result, skip_out, left_side, joining)

        def forward_resting(operands):
            return (blank, blank, blank, blank)

        result, skip_out, left_side, joining = lax.cond(
            active_tick, forward_compute, forward_resting, (arriving, skip_here)
        )
        left_buffer = put_slot(left_buffer, slot_index, left_side, active_tick)
        input_buffer = put_slot(input_buffer, slot_index, joining, active_tick)
        incoming = passed_along(result, "section", 1)
        if sending:
            arrived = mirror_forward(skip_out, sections)
            source = tick_index - (sections - 1 - position)
            landing = is_deep & (source >= 0) & (source < micro_count)
            skip_buffer = put_slot(
                skip_buffer, jnp.clip(source, 0, micro_count - 1), arrived, landing
            )
        return (incoming, skip_buffer, left_buffer, input_buffer)

    first_phase = halfway + micro_count - 1
    forward_state = (blank, blank_stack, blank_stack, blank_stack)
    forward_state = lax.fori_loop(
        0, first_phase, lambda t, c: forward_tick(t, c, True), forward_state
    )
    forward_state = lax.fori_loop(
        first_phase, first_phase + halfway, lambda t, c: forward_tick(t, c, False), forward_state
    )
    unused_in, unused_skip, left_buffer, input_buffer = forward_state
    up_back, down_back, join_back = (up_full, down_full, join_full)

    def backward_tick(tick_index, carried_state, sending):
        (
            incoming,
            turn_buffer,
            scaled_buffer,
            active_buffer,
            pre_buffer,
            cot_buffer,
            right_buffer,
        ) = carried_state
        micro_index = tick_index - (sections - 1 - position)
        active_tick = (micro_index >= 0) & (micro_index < micro_count)
        slot_index = jnp.clip(micro_index, 0, micro_count - 1)
        arriving = jnp.where(position == sections - 1, cotangent[slot_index], incoming)
        turned = lax.dynamic_index_in_dim(turn_buffer, slot_index, 0, keepdims=False)
        block_in = lax.dynamic_index_in_dim(input_buffer, slot_index, 0, keepdims=False)

        def backward_compute(operands):
            stream_in, turned_in, mixture = operands
            cotangent_in = lax.cond(
                is_deep,
                lambda: stream_in,
                lambda: (
                    stream_in.astype(jnp.float32)
                    + jnp.dot(turned_in, join_back.T, preferred_element_type=jnp.float32)
                ).astype(jnp.bfloat16),
            )
            grad_input, scaled, active, grad_pre = block_backward(
                mixture, gain_row, up_back, down_back, cotangent_in
            )
            passed = lax.cond(
                is_deep,
                lambda: jnp.dot(grad_input, join_back.T, preferred_element_type=jnp.float32).astype(
                    jnp.bfloat16
                ),
                lambda: grad_input,
            )
            right_side = jnp.where(is_deep, grad_input, turned_in)
            skip_back = jnp.where(is_deep, grad_input, jnp.zeros_like(grad_input))
            return (passed, skip_back, scaled, active, grad_pre, cotangent_in, right_side)

        def backward_resting(operands):
            wide_blank = jnp.zeros((row_count, up_back.shape[1]), jnp.bfloat16)
            return (blank, blank, blank, wide_blank, wide_blank, blank, blank)

        passed, skip_back, scaled, active, grad_pre, cotangent_in, right_side = lax.cond(
            active_tick, backward_compute, backward_resting, (arriving, turned, block_in)
        )
        scaled_buffer = put_slot(scaled_buffer, slot_index, scaled, active_tick)
        active_buffer = put_slot(active_buffer, slot_index, active, active_tick)
        pre_buffer = put_slot(pre_buffer, slot_index, grad_pre, active_tick)
        cot_buffer = put_slot(cot_buffer, slot_index, cotangent_in, active_tick)
        right_buffer = put_slot(right_buffer, slot_index, right_side, active_tick)
        incoming = passed_along(passed, "section", -1)
        if sending:
            arrived = mirror_backward(skip_back, sections)
            source = tick_index - position
            landing = jnp.logical_not(is_deep) & (source >= 0) & (source < micro_count)
            turn_buffer = put_slot(
                turn_buffer, jnp.clip(source, 0, micro_count - 1), arrived, landing
            )
        return (
            incoming,
            turn_buffer,
            scaled_buffer,
            active_buffer,
            pre_buffer,
            cot_buffer,
            right_buffer,
        )

    backward_state = (
        blank,
        blank_stack,
        blank_stack,
        wide_stack,
        wide_stack,
        blank_stack,
        blank_stack,
    )
    backward_state = lax.fori_loop(
        0, first_phase, lambda t, c: backward_tick(t, c, True), backward_state
    )
    backward_state = lax.fori_loop(
        first_phase, first_phase + halfway, lambda t, c: backward_tick(t, c, False), backward_state
    )
    unused_cot, unused_turn, scaled_buffer, active_buffer, pre_buffer, cot_buffer, right_buffer = (
        backward_state
    )
    token_count = micro_count * row_count

    def flatten(buffer):
        return buffer.reshape(token_count, buffer.shape[2])

    grad_up = jnp.dot(
        flatten(scaled_buffer).T, flatten(pre_buffer), preferred_element_type=jnp.float32
    )
    grad_down = jnp.dot(
        flatten(active_buffer).T, flatten(cot_buffer), preferred_element_type=jnp.float32
    )
    grad_join = jnp.dot(
        flatten(left_buffer).T, flatten(right_buffer), preferred_element_type=jnp.float32
    )
    summed_up, summed_down, summed_join = (
        lax.psum_scatter(
            grad_up[None].astype(jnp.bfloat16), "dp", scatter_dimension=1, tiled=True
        ).astype(jnp.float32),
        lax.psum_scatter(
            grad_down[None].astype(jnp.bfloat16), "dp", scatter_dimension=1, tiled=True
        ).astype(jnp.float32),
        lax.psum_scatter(
            grad_join[None].astype(jnp.bfloat16), "dp", scatter_dimension=1, tiled=True
        ).astype(jnp.float32),
    )
    return (summed_up, summed_down, summed_join)


def solution(mesh):
    in_specs = (
        P(None, "dp", None),
        P(),
        P(),
        P(),
        P("section", None),
        P("section", "dp", None),
        P("section", "dp", None),
        P("section", "dp", None),
        P(None, "dp", None),
    )
    out_specs = (P("section", "dp", None), P("section", "dp", None), P("section", "dp", None))
    return jax.shard_map(local, mesh=mesh, in_specs=in_specs, out_specs=out_specs, check_vma=False)
```

profile of v0, /device:TPU:32, one launch (start us, length us, event | category | flops | bytes accessed | tf_op | source)
XLA Modules:
  0.0 1370.3 jit_solution(12019182642807131170)
XLA Ops:
  12.4 158.6 %all-gather.4.cloned.1.call-done = bf16[1,1152,1152]{2,0,1:T(2,128)(2,1)} async-done(((bf16[1,36,1152]{2,0,1:T(2,128)(2,1)}), bf16[1,1152,1152]{2,0,1:T(2,128)(2,1)}) %all-gather.4.cloned.1.call-update) | async-done | bytes 2654224 | tf_op jit(solution)/shard_map/all_gather | solution.py:93
  174.0 173.1 %all-gather.8.cloned.1.call-done = bf16[1,1152,2304]{2,0,1:T(2,128)(2,1)} async-done(((bf16[1,36,2304]{2,0,1:T(2,128)(2,1)}), bf16[1,1152,2304]{2,0,1:T(2,128)(2,1)}) %all-gather.8.cloned.1.call-update) | async-done | bytes 5308432 | tf_op jit(solution)/shard_map/all_gather | solution.py:91
  354.3 156.6 %all-gather.6.cloned.1.call-done = bf16[1,2304,1152]{2,1,0:T(8,128)(2,1)} async-done(((bf16[1,72,1152]{2,1,0:T(8,128)(2,1)}), bf16[1,2304,1152]{2,1,0:T(8,128)(2,1)}) %all-gather.6.cloned.1.call-update) | async-done | bytes 5308432 | tf_op jit(solution)/shard_map/all_gather | solution.py:92
  511.8 196.8 %while.89 = (s32[]{:T(128)}, bf16[64,1152]{1,0:T(8,128)(2,1)S(1)}, bf16[2,64,1152]{2,1,0:T(8,128)(2,1)S(1)}, bf16[2,64,1152]{2,1,0:T(8,128)(2,1)}, bf16[2,64,115...) while((s32[]{:T(128)}, bf16[64,1152]{1,0:T(8,128)(2,1)S(1)}, ...), condition=%wide.region_9.10_spmd, body=%wide.region_0.9_spmd.sunk | while | flops 1022462272 | bytes 22882380 | solution.py:156
  518.7 11.8 conditional.15
  540.7 12.2 collective-permute-done.3
  559.8 11.8 conditional.15
  581.8 12.2 collective-permute-done.3
  621.5 13.0 collective-permute-done.3
  660.1 13.8 %collective-permute-done.3 = bf16[64,1152]{1,0:T(8,128)(2,1)S(1)} collective-permute-done((bf16[64,1152]{1,0:T(8,128)(2,1)}, bf16[64,1152]{1,0:T(8,128)(2,1)S(1)}, u32[]{:S(2)}, u32[]{:S(2)}) %collective-permute-start.3) | collective-permute-done | bytes 147488 | tf_op jit(solution)/shard_map/while/body/eval_jaxpr/ppermute | solution.py:16
  708.6 66.7 %while.90 = (s32[]{:T(128)}, bf16[64,1152]{1,0:T(8,128)(2,1)S(1)}, bf16[2,64,1152]{2,1,0:T(8,128)(2,1)}, bf16[2,64,1152]{2,1,0:T(8,128)(2,1)S(1)}, s32[]{:T(128)...) while((s32[]{:T(128)}, bf16[64,1152]{1,0:T(8,128)(2,1)S(1)}, ...), condition=%wide.region_17.18_spmd, body=%wide.region_10.17_spmd.sunk | while | flops 852445504 | bytes 17426352 | solution.py:159
  730.5 9.9 collective-permute-start.4
  779.3 242.4 %while.91 = (s32[]{:T(128)}, bf16[64,1152]{1,0:T(8,128)(2,1)S(1)}, bf16[2,64,1152]{2,1,0:T(8,128)(2,1)S(1)}, bf16[2,64,1152]{2,1,0:T(8,128)(2,1)}, bf16[2,64,230...) while((s32[]{:T(128)}, bf16[64,1152]{1,0:T(8,128)(2,1)S(1)}, ...), condition=%wide.region_29.30_spmd, body=%wide.region_18.29_spmd.sunk | while | flops 1365369984 | bytes 58566008 | solution.py:245
  808.0 25.6 %collective-permute-start.8 = (bf16[64,1152]{1,0:T(8,128)(2,1)}, bf16[64,1152]{1,0:T(8,128)(2,1)}, u32[]{:S(2)}, u32[]{:S(2)}) collective-permute-start(bf16[64,1152]{1,0:T(8,128)(2,1)} %collective-permute-done.7), channel_id=1, source_target_pairs={{0,4},{4,0},{1,5},{5,1},{2,6},{6,2},{3,7},{7,3},{8,12},{12,8},{9,1... | collective-permute-start | bytes 442376 | tf_op jit(solution)/shard_map/while/body/eval_jaxpr/ppermute | solution.py:16
  861.0 18.5 %collective-permute-start.8 = (bf16[64,1152]{1,0:T(8,128)(2,1)}, bf16[64,1152]{1,0:T(8,128)(2,1)}, u32[]{:S(2)}, u32[]{:S(2)}) collective-permute-start(bf16[64,1152]{1,0:T(8,128)(2,1)} %collective-permute-done.7), channel_id=1, source_target_pairs={{0,4},{4,0},{1,5},{5,1},{2,6},{6,2},{3,7},{7,3},{8,12},{12,8},{9,1... | collective-permute-start | bytes 442376 | tf_op jit(solution)/shard_map/while/body/eval_jaxpr/ppermute | solution.py:16
  907.6 18.0 %collective-permute-start.8 = (bf16[64,1152]{1,0:T(8,128)(2,1)}, bf16[64,1152]{1,0:T(8,128)(2,1)}, u32[]{:S(2)}, u32[]{:S(2)}) collective-permute-start(bf16[64,1152]{1,0:T(8,128)(2,1)} %collective-permute-done.7), channel_id=1, source_target_pairs={{0,4},{4,0},{1,5},{5,1},{2,6},{6,2},{3,7},{7,3},{8,12},{12,8},{9,1... | collective-permute-start | bytes 442376 | tf_op jit(solution)/shard_map/while/body/eval_jaxpr/ppermute | solution.py:16
  952.4 19.3 %collective-permute-start.8 = (bf16[64,1152]{1,0:T(8,128)(2,1)}, bf16[64,1152]{1,0:T(8,128)(2,1)}, u32[]{:S(2)}, u32[]{:S(2)}) collective-permute-start(bf16[64,1152]{1,0:T(8,128)(2,1)} %collective-permute-done.7), channel_id=1, source_target_pairs={{0,4},{4,0},{1,5},{5,1},{2,6},{6,2},{3,7},{7,3},{8,12},{12,8},{9,1... | collective-permute-start | bytes 442376 | tf_op jit(solution)/shard_map/while/body/eval_jaxpr/ppermute | solution.py:16
  1002.5 14.7 %collective-permute-start.8 = (bf16[64,1152]{1,0:T(8,128)(2,1)}, bf16[64,1152]{1,0:T(8,128)(2,1)}, u32[]{:S(2)}, u32[]{:S(2)}) collective-permute-start(bf16[64,1152]{1,0:T(8,128)(2,1)} %collective-permute-done.7), channel_id=1, source_target_pairs={{0,4},{4,0},{1,5},{5,1},{2,6},{6,2},{3,7},{7,3},{8,12},{12,8},{9,1... | collective-permute-start | bytes 442376 | tf_op jit(solution)/shard_map/while/body/eval_jaxpr/ppermute | solution.py:16
  1021.7 96.0 %while.92 = (s32[]{:T(128)}, bf16[64,1152]{1,0:T(8,128)(2,1)S(1)}, bf16[2,64,1152]{2,1,0:T(8,128)(2,1)}, bf16[2,64,2304]{2,1,0:T(8,128)(2,1)}, bf16[2,64,2304]{2...) while((s32[]{:T(128)}, bf16[64,1152]{1,0:T(8,128)(2,1)S(1)}, ...), condition=%wide.region_41.42_spmd, body=%wide.region_30.41_spmd.sunk | while | flops 1365222528 | bytes 56059068 | solution.py:248
  1045.9 17.0 %collective-permute-done.9 = bf16[64,1152]{1,0:T(8,128)(2,1)S(1)} collective-permute-done((bf16[64,1152]{1,0:T(8,128)(2,1)}, bf16[64,1152]{1,0:T(8,128)(2,1)S(1)}, u32[]{:S(2)}, u32[]{:S(2)}) %collective-permute-start.9) | collective-permute-done | bytes 147488 | tf_op jit(solution)/shard_map/while/body/eval_jaxpr/ppermute | solution.py:22
  1062.9 15.7 %conditional.18 = (bf16[64,1152]{1,0:T(8,128)(2,1)}, bf16[64,1152]{1,0:T(8,128)(2,1)}, bf16[64,2304]{1,0:T(8,128)(2,1)}, bf16[64,2304]{1,0:T(8,128)(2,1)}, bf16[...) conditional(s32[]{:T(128)} %convert_element_type.502, () %tuple.308, (pred[]{:T(512)}, pred[]{:T(512)}, ...), branch_computations={%region_31.31_spmd, %region_32.40_spmd} | conditional | flops 1364706432 | bytes 50306336 | solution.py:210
  1090.6 15.7 %conditional.18 = (bf16[64,1152]{1,0:T(8,128)(2,1)}, bf16[64,1152]{1,0:T(8,128)(2,1)}, bf16[64,2304]{1,0:T(8,128)(2,1)}, bf16[64,2304]{1,0:T(8,128)(2,1)}, bf16[...) conditional(s32[]{:T(128)} %convert_element_type.502, () %tuple.308, (pred[]{:T(512)}, pred[]{:T(512)}, ...), branch_computations={%region_31.31_spmd, %region_32.40_spmd} | conditional | flops 1364706432 | bytes 50306336 | solution.py:210
  1129.5 177.7 %fusion.126 = (bf16[40,2304]{1,0:T(8,128)(2,1)S(1)}, bf16[48,1152]{1,0:T(8,128)(2,1)S(1)}) fusion(bf16[1,1152,2304]{2,1,0:T(8,128)(2,1)} %fusion.121, bf16[1,1152,1152]{2,1,0:T(8,128)(2,1)S(1)} %copy-done.9), kind=kCustom, calls=%all-reduce-scatter.2 | all-reduce-scatter fusion | flops 4718594 | bytes 8258560
  1329.1 9.2 collective-permute-start.19
  (497 shorter events, 521.7 us)
Async XLA Ops:
  7.2 163.9 %all-gather.4.cloned.1.call-start = ((), (), s32[]{:S(2)}) async-start(), calls=%async_computation.1 | async-start | bytes 5474304 | tf_op jit(solution)/shard_map/all_gather | solution.py:93
  8.9 338.2 %all-gather.8.cloned.1.call-start = ((), (), s32[]{:S(2)}) async-start(), calls=%async_computation.3 | async-start | bytes 10948608 | tf_op jit(solution)/shard_map/all_gather | solution.py:91
  10.9 500.1 %all-gather.6.cloned.1.call-start = ((), (), s32[]{:S(2)}) async-start(), calls=%async_computation.2 | async-start | bytes 5474304 | tf_op jit(solution)/shard_map/all_gather | solution.py:92
  11.6 1350.5 %reduce-scatter.12.cloned.1.call-start = ((), (), s32[]{:S(2)}) async-start(), calls=%async_computation.4 | async-start | bytes 5474304
  530.5 22.5 %collective-permute-start = (bf16[64,1152]{1,0:T(8,128)(2,1)}, bf16[64,1152]{1,0:T(8,128)(2,1)S(1)}, u32[]{:S(2)}, u32[]{:S(2)}) collective-permute-start(bf16[64,1152]{1,0:T(8,128)(2,1)} %get-tuple-element.2432), channel_id=1, source_target_pairs={{0,1},{1,2},{2,3},{3,4},{4,5},{5,6},{6,7},{8,9},{9,10},{10,11},{11... | collective-permute-start | bytes 442376 | tf_op jit(solution)/shard_map/while/body/eval_jaxpr/ppermute | solution.py:22
  571.6 22.5 %collective-permute-start = (bf16[64,1152]{1,0:T(8,128)(2,1)}, bf16[64,1152]{1,0:T(8,128)(2,1)S(1)}, u32[]{:S(2)}, u32[]{:S(2)}) collective-permute-start(bf16[64,1152]{1,0:T(8,128)(2,1)} %get-tuple-element.2432), channel_id=1, source_target_pairs={{0,1},{1,2},{2,3},{3,4},{4,5},{5,6},{6,7},{8,9},{9,10},{10,11},{11... | collective-permute-start | bytes 442376 | tf_op jit(solution)/shard_map/while/body/eval_jaxpr/ppermute | solution.py:22
  610.9 23.6 %collective-permute-start = (bf16[64,1152]{1,0:T(8,128)(2,1)}, bf16[64,1152]{1,0:T(8,128)(2,1)S(1)}, u32[]{:S(2)}, u32[]{:S(2)}) collective-permute-start(bf16[64,1152]{1,0:T(8,128)(2,1)} %get-tuple-element.2432), channel_id=1, source_target_pairs={{0,1},{1,2},{2,3},{3,4},{4,5},{5,6},{6,7},{8,9},{9,10},{10,11},{11... | collective-permute-start | bytes 442376 | tf_op jit(solution)/shard_map/while/body/eval_jaxpr/ppermute | solution.py:22
  644.0 29.9 %collective-permute-start = (bf16[64,1152]{1,0:T(8,128)(2,1)}, bf16[64,1152]{1,0:T(8,128)(2,1)S(1)}, u32[]{:S(2)}, u32[]{:S(2)}) collective-permute-start(bf16[64,1152]{1,0:T(8,128)(2,1)} %get-tuple-element.2432), channel_id=1, source_target_pairs={{0,1},{1,2},{2,3},{3,4},{4,5},{5,6},{6,7},{8,9},{9,10},{10,11},{11... | collective-permute-start | bytes 442376 | tf_op jit(solution)/shard_map/while/body/eval_jaxpr/ppermute | solution.py:22
  683.5 25.1 %collective-permute-start = (bf16[64,1152]{1,0:T(8,128)(2,1)}, bf16[64,1152]{1,0:T(8,128)(2,1)S(1)}, u32[]{:S(2)}, u32[]{:S(2)}) collective-permute-start(bf16[64,1152]{1,0:T(8,128)(2,1)} %get-tuple-element.2432), channel_id=1, source_target_pairs={{0,1},{1,2},{2,3},{3,4},{4,5},{5,6},{6,7},{8,9},{9,10},{10,11},{11... | collective-permute-start | bytes 442376 | tf_op jit(solution)/shard_map/while/body/eval_jaxpr/ppermute | solution.py:22
  787.6 51.0 %collective-permute-start.5 = (bf16[64,1152]{1,0:T(8,128)(2,1)}, bf16[64,1152]{1,0:T(8,128)(2,1)S(1)}, u32[]{:S(2)}, u32[]{:S(2)}) collective-permute-start(bf16[64,1152]{1,0:T(8,128)(2,1)} %get-tuple-element.2478), channel_id=1, source_target_pairs={{1,0},{2,1},{3,2},{4,3},{5,4},{6,5},{7,6},{9,8},{10,9},{11,10},{12... | collective-permute-start | bytes 442376 | tf_op jit(solution)/shard_map/while/body/eval_jaxpr/ppermute | solution.py:22
  808.0 29.7 %collective-permute-start.8 = (bf16[64,1152]{1,0:T(8,128)(2,1)}, bf16[64,1152]{1,0:T(8,128)(2,1)}, u32[]{:S(2)}, u32[]{:S(2)}) collective-permute-start(bf16[64,1152]{1,0:T(8,128)(2,1)} %collective-permute-done.7), channel_id=1, source_target_pairs={{0,4},{4,0},{1,5},{5,1},{2,6},{6,2},{3,7},{7,3},{8,12},{12,8},{9,1... | collective-permute-start | bytes 442376 | tf_op jit(solution)/shard_map/while/body/eval_jaxpr/ppermute | solution.py:16
  845.9 42.2 %collective-permute-start.5 = (bf16[64,1152]{1,0:T(8,128)(2,1)}, bf16[64,1152]{1,0:T(8,128)(2,1)S(1)}, u32[]{:S(2)}, u32[]{:S(2)}) collective-permute-start(bf16[64,1152]{1,0:T(8,128)(2,1)} %get-tuple-element.2478), channel_id=1, source_target_pairs={{1,0},{2,1},{3,2},{4,3},{5,4},{6,5},{7,6},{9,8},{10,9},{11,10},{12... | collective-permute-start | bytes 442376 | tf_op jit(solution)/shard_map/while/body/eval_jaxpr/ppermute | solution.py:22
  861.0 26.1 %collective-permute-start.8 = (bf16[64,1152]{1,0:T(8,128)(2,1)}, bf16[64,1152]{1,0:T(8,128)(2,1)}, u32[]{:S(2)}, u32[]{:S(2)}) collective-permute-start(bf16[64,1152]{1,0:T(8,128)(2,1)} %collective-permute-done.7), channel_id=1, source_target_pairs={{0,4},{4,0},{1,5},{5,1},{2,6},{6,2},{3,7},{7,3},{8,12},{12,8},{9,1... | collective-permute-start | bytes 442376 | tf_op jit(solution)/shard_map/while/body/eval_jaxpr/ppermute | solution.py:16
  892.3 40.1 %collective-permute-start.5 = (bf16[64,1152]{1,0:T(8,128)(2,1)}, bf16[64,1152]{1,0:T(8,128)(2,1)S(1)}, u32[]{:S(2)}, u32[]{:S(2)}) collective-permute-start(bf16[64,1152]{1,0:T(8,128)(2,1)} %get-tuple-element.2478), channel_id=1, source_target_pairs={{1,0},{2,1},{3,2},{4,3},{5,4},{6,5},{7,6},{9,8},{10,9},{11,10},{12... | collective-permute-start | bytes 442376 | tf_op jit(solution)/shard_map/while/body/eval_jaxpr/ppermute | solution.py:22
  907.6 24.7 %collective-permute-start.8 = (bf16[64,1152]{1,0:T(8,128)(2,1)}, bf16[64,1152]{1,0:T(8,128)(2,1)}, u32[]{:S(2)}, u32[]{:S(2)}) collective-permute-start(bf16[64,1152]{1,0:T(8,128)(2,1)} %collective-permute-done.7), channel_id=1, source_target_pairs={{0,4},{4,0},{1,5},{5,1},{2,6},{6,2},{3,7},{7,3},{8,12},{12,8},{9,1... | collective-permute-start | bytes 442376 | tf_op jit(solution)/shard_map/while/body/eval_jaxpr/ppermute | solution.py:16
  937.4 42.2 %collective-permute-start.5 = (bf16[64,1152]{1,0:T(8,128)(2,1)}, bf16[64,1152]{1,0:T(8,128)(2,1)S(1)}, u32[]{:S(2)}, u32[]{:S(2)}) collective-permute-start(bf16[64,1152]{1,0:T(8,128)(2,1)} %get-tuple-element.2478), channel_id=1, source_target_pairs={{1,0},{2,1},{3,2},{4,3},{5,4},{6,5},{7,6},{9,8},{10,9},{11,10},{12... | collective-permute-start | bytes 442376 | tf_op jit(solution)/shard_map/while/body/eval_jaxpr/ppermute | solution.py:22
  952.4 27.2 %collective-permute-start.8 = (bf16[64,1152]{1,0:T(8,128)(2,1)}, bf16[64,1152]{1,0:T(8,128)(2,1)}, u32[]{:S(2)}, u32[]{:S(2)}) collective-permute-start(bf16[64,1152]{1,0:T(8,128)(2,1)} %collective-permute-done.7), channel_id=1, source_target_pairs={{0,4},{4,0},{1,5},{5,1},{2,6},{6,2},{3,7},{7,3},{8,12},{12,8},{9,1... | collective-permute-start | bytes 442376 | tf_op jit(solution)/shard_map/while/body/eval_jaxpr/ppermute | solution.py:16
  983.8 37.9 %collective-permute-start.5 = (bf16[64,1152]{1,0:T(8,128)(2,1)}, bf16[64,1152]{1,0:T(8,128)(2,1)S(1)}, u32[]{:S(2)}, u32[]{:S(2)}) collective-permute-start(bf16[64,1152]{1,0:T(8,128)(2,1)} %get-tuple-element.2478), channel_id=1, source_target_pairs={{1,0},{2,1},{3,2},{4,3},{5,4},{6,5},{7,6},{9,8},{10,9},{11,10},{12... | collective-permute-start | bytes 442376 | tf_op jit(solution)/shard_map/while/body/eval_jaxpr/ppermute | solution.py:22
  1037.3 25.5 %collective-permute-start.9 = (bf16[64,1152]{1,0:T(8,128)(2,1)}, bf16[64,1152]{1,0:T(8,128)(2,1)S(1)}, u32[]{:S(2)}, u32[]{:S(2)}) collective-permute-start(bf16[64,1152]{1,0:T(8,128)(2,1)} %get-tuple-element.2508), channel_id=1, source_target_pairs={{1,0},{2,1},{3,2},{4,3},{5,4},{6,5},{7,6},{9,8},{10,9},{11,10},{12... | collective-permute-start | bytes 442376 | tf_op jit(solution)/shard_map/while/body/eval_jaxpr/ppermute | solution.py:22
  1307.1 22.0 %collective-permute-start.14 = (bf16[48,1152]{1,0:T(8,128)(2,1)S(1)}, bf16[48,1152]{1,0:T(8,128)(2,1)S(1)}, u32[]{:S(2)}, u32[]{:S(2)}) collective-permute-start(bf16[48,1152]{1,0:T(8,128)(2,1)S(1)} %get-tuple-element.1995), channel_id=1, source_target_pairs={{0,8},{8,16},{16,24},{24,32},{32,40},{40,48},{48,56},{56,64},{64,7... | collective-permute-start | bytes 331784
  1313.0 25.3 %collective-permute-start.15 = (bf16[48,1152]{1,0:T(8,128)(2,1)S(1)}, bf16[48,1152]{1,0:T(8,128)(2,1)S(1)}, u32[]{:S(2)}, u32[]{:S(2)}) collective-permute-start(bf16[48,1152]{1,0:T(8,128)(2,1)S(1)} %get-tuple-element.1995), channel_id=1, source_target_pairs={{0,16},{8,24},{16,32},{24,40},{32,48},{40,56},{48,64},{56,72},{64,... | collective-permute-start | bytes 331784
  1319.1 23.4 %collective-permute-start.16 = (bf16[48,1152]{1,0:T(8,128)(2,1)S(1)}, bf16[48,1152]{1,0:T(8,128)(2,1)S(1)}, u32[]{:S(2)}, u32[]{:S(2)}) collective-permute-start(bf16[48,1152]{1,0:T(8,128)(2,1)S(1)} %get-tuple-element.1995), channel_id=1, source_target_pairs={{0,24},{8,32},{16,40},{24,48},{32,56},{40,64},{48,72},{56,80},{64,... | collective-permute-start | bytes 331784
  1326.7 21.7 %collective-permute-start.18 = (bf16[48,1152]{1,0:T(8,128)(2,1)S(1)}, bf16[48,1152]{1,0:T(8,128)(2,1)S(1)}, u32[]{:S(2)}, u32[]{:S(2)}) collective-permute-start(bf16[48,1152]{1,0:T(8,128)(2,1)S(1)} %get-tuple-element.1995), channel_id=1, source_target_pairs={{0,40},{8,48},{16,56},{24,64},{32,72},{40,80},{48,88},{56,96},{64,... | collective-permute-start | bytes 331784
  1329.1 25.0 %collective-permute-start.19 = (bf16[48,1152]{1,0:T(8,128)(2,1)S(1)}, bf16[48,1152]{1,0:T(8,128)(2,1)S(1)}, u32[]{:S(2)}, u32[]{:S(2)}) collective-permute-start(bf16[48,1152]{1,0:T(8,128)(2,1)S(1)} %get-tuple-element.1995), channel_id=1, source_target_pairs={{0,48},{8,56},{16,64},{24,72},{32,80},{40,88},{48,96},{56,104},{64... | collective-permute-start | bytes 331784
  (71 other events, 1577.6 us)
Sparse Core Ops, SparseCore 0:
  10.4 160.6 all-gather.3
  173.4 173.6 all-gather.7
  348.9 161.9 all-gather.5
  1123.0 209.2 reduce-scatter.11
where the time goes:
time: 1370 us
  waiting for transfers between devices  632 us (46%)
  starting transfers between devices  255 us (19%)
  blocking collectives  178 us (13%)
  local copies, waits for them, and re-layouts  132 us (10%)
  other arithmetic  69 us (5%)
  matrix products  52.7 us (4%)
  loops' own time  37 us (3%)
  between operations  15.4 us (1%)
    unnamed x1, blocking collectives  178 us
    all_gather x1, waiting for transfers between devices, local(): lax.all_gather(w_up, 'dp', axis=1, tiled=True)  173 us
    ppermute x30, starting transfers between devices, from_partner(): return lax.ppermute(block, axis, route)  160 us
    all_gather x1, waiting for transfers between devices, local(): lax.all_gather(w_join, 'dp', axis=1, tiled=True)  159 us
    all_gather x1, waiting for transfers between devices, local(): lax.all_gather(w_down, 'dp', axis=1, tiled=True)  157 us
    ppermute x30, waiting for transfers between devices, from_partner(): return lax.ppermute(block, axis, route)  124 us
    dynamic_slice x68, local copies, waits for them, and re-layouts, put_slot(): current = lax.dynamic_index_in_dim(buffer, slot_index, 0, keepdims=False)  51.4 us
    ppermute x18, starting transfers between devices, passed_along(): return lax.ppermute(x, axis, pairs)  47.3 us
  transfers between devices with their start and end apart: 64, of which 26 were waited for; matrix products, arithmetic and copies ran while one was open for 21% of the time, Pallas kernels for 0%

commit v1 on v0

v1 whole, which is shorter than its diff:
```python
import functools

import jax
import jax.numpy as jnp
from jax import lax
from jax.experimental import pallas as pl
from jax.experimental.pallas import tpu as pltpu
from jax.sharding import PartitionSpec as P

BF = jnp.bfloat16
F32 = jnp.float32
EPSILON = 1e-06
MESH = pl.DeviceIdType.MESH
D = 1152
FFW = 2304
ROWS = 64
DIRS = ((1, 8), (-1, 7))
PART = (((0, 5), (5, 4)), ((0, 4), (4, 5)), ((0, 4), (4, 5)))
UNIT = ((4, FFW), (8, D), (4, D))
GELU_C = 0.7978845608028654
GELU_A = 0.044715


def rem(a, b):
    return lax.rem(a, jnp.int32(b))


def div(a, b):
    return lax.div(a, jnp.int32(b))


def cycle_xy(h, t):
    a = div(t, 4)
    b = rem(t + 16 - a, 4)
    return (a, b) if h == 0 else (b, a)


def dot(a, b):
    return jnp.dot(a, b, preferred_element_type=F32)


def dot_nt(a, b):
    return lax.dot_general(a, b, (((1,), (1,)), ((), ())), preferred_element_type=F32)


def await_bytes(ref, sem):
    pltpu.make_async_copy(ref, ref, sem).wait()


def kernel(
    up_in, dn_in, jn_in, gain_in, ent_in, cot_in,
    up_out, dn_out, jn_out,
    g_up, g_dn, g_jn, w_up, w_dn, w_jn, rx_up, rx_dn, rx_jn, rr_up, rr_dn, rr_jn,
    fo_up, fo_dn, fo_jn, gain, hin, skin, cin, tin, u_s, hout, skout, cout, gout,
    scaled_s, active_s, dg_s, gp_s, e_s, normed_s, inv_s, right_s, lt, at,
    swap_sem, swap_send, io_send, ag_recv, ag_send, f_recv, f_send,
    act_recv, act_send, x_recv, x_send, rs_recv, rs_send, o_recv, o_send,
):
    q = lax.axis_index("dp")
    s = lax.axis_index("section")
    x, zl, y = div(q, 8), rem(div(q, 4), 2), rem(q, 4)
    zh, c = div(s, 2), rem(s, 2)
    z = 2 * zh + zl
    deep = z >= 4

    def device(xx, yy, zz, cc):
        return (xx * 8 + rem(zz, 2) * 4 + yy, div(zz, 2) * 2 + cc)

    partner = device(x, y, z, 1 - c)
    z_up = device(x, y, rem(z + 1, 8), c)
    z_down = device(x, y, rem(z + 7, 8), c)
    mirror = device(x, y, 7 - z, c)
    swap = device(x, y, 2 * zh + c, zl)
    stays = zl == c
    pos = (4 * x + rem(x + y, 4), 4 * y + rem(x + y, 4))

    def neighbour(h, d):
        xx, yy = cycle_xy(h, rem(pos[h] + 16 + d, 16))
        return device(xx, yy, z, c)

    def slot_of(h, t, cls):
        xx, yy = cycle_xy(h, t)
        return xx * 8 + cls * 4 + yy

    ring = tuple(tuple(neighbour(h, d) for d, _ in DIRS) for h in range(2))
    other = device(x, y, rem(z, 2) * 0 + 2 * zh + 1 - zl, 1 - c)

    barrier = pltpu.get_barrier_semaphore()
    greet = [ring[0][0], ring[0][1], ring[1][0], ring[1][1], partner, z_up, z_down, mirror, other]
    for peer in greet:
        pl.semaphore_signal(barrier, inc=1, device_id=peer, device_id_type=MESH)
    pl.semaphore_wait(barrier, len(greet))

    gs = (g_up, g_dn, g_jn)
    rxs = (rx_up, rx_dn, rx_jn)
    rrs = (rr_up, rr_dn, rr_jn)
    fos = (fo_up, fo_dn, fo_jn)
    outs = (up_out, dn_out, jn_out)

    def remote(src, dst, send, recv, dev):
        return pltpu.make_async_remote_copy(
            src_ref=src, dst_ref=dst, send_sem=send, recv_sem=recv, device_id=dev, device_id_type=MESH
        )

    def swap_copy(src, dst, send, recv):
        @pl.when(stays)
        def _():
            pltpu.make_async_copy(src, dst, recv).start()

        @pl.when(jnp.logical_not(stays))
        def _():
            remote(src, dst, send, recv, swap).start()

    def swap_sent(src, send):
        @pl.when(jnp.logical_not(stays))
        def _():
            await_bytes(src, send)

    ins = (up_in, dn_in, jn_in)
    for m in range(3):
        swap_copy(ins[m], gs[m].at[pl.ds(9 * q, 9)], swap_send.at[m], swap_sem.at[m])
    swap_copy(gain_in, gain, swap_send.at[3], swap_sem.at[3])
    gives_entry = (zh == 0) & (c == 0)
    gives_cot = (zh == 3) & (c == 1)

    @pl.when(gives_entry)
    def _():
        for i in range(2):
            swap_copy(ent_in.at[i], hin.at[i], io_send.at[0, i], act_recv.at[0, i])

    @pl.when(gives_cot)
    def _():
        for i in range(2):
            swap_copy(cot_in.at[i], cin.at[i], io_send.at[1, i], act_recv.at[2, i])

    own = x * 8 + c * 4 + y
    for m in range(3):
        await_bytes(gs[m].at[pl.ds(9 * own, 9)], swap_sem.at[m])

    def chunk(m, h, t):
        off, cnt = PART[m][h]
        return gs[m].at[pl.ds(9 * slot_of(h, t, c) + off, cnt)]

    def ag_step(k, _):
        for m in range(3):
            for h in range(2):
                for di, (d, n) in enumerate(DIRS):
                    @pl.when(k < n)
                    def _():
                        ref = chunk(m, h, rem(pos[h] + 16 - d * k, 16))

                        @pl.when(k > 0)
                        def _():
                            await_bytes(ref, ag_recv.at[m, h, di, lax.max(k - 1, 0)])

                        remote(ref, ref, ag_send.at[m], ag_recv.at[m, h, di, k], ring[h][di]).start()
                        if di == 0:
                            remote(ref, ref, f_send.at[m], f_recv.at[m], partner).start()
                        else:
                            @pl.when(k > 0)
                            def _():
                                remote(ref, ref, f_send.at[m], f_recv.at[m], partner).start()
        return 0

    lax.fori_loop(0, 8, ag_step, 0)
    for m in range(3):
        for h in range(2):
            for di, (d, n) in enumerate(DIRS):
                ref = chunk(m, h, rem(pos[h] + 16 - d * n, 16))
                await_bytes(ref, ag_recv.at[m, h, di, n - 1])
                remote(ref, ref, f_send.at[m], f_recv.at[m], partner).start()
    for m in range(3):
        await_bytes(gs[m].at[pl.ds(0, 144)], f_recv.at[m])

    def conv_up(t, _):
        w_up[pl.ds(pl.multiple_of(t * 16, 16), 16), :] = g_up[pl.ds(t * 4, 4)].reshape(16, FFW)
        return 0

    def conv_dn(t, _):
        w_dn[pl.ds(pl.multiple_of(t * 32, 32), 32), :] = g_dn[pl.ds(t * 4, 4)].reshape(32, D)
        return 0

    def conv_jn(t, _):
        w_jn[pl.ds(pl.multiple_of(t * 16, 16), 16), :] = g_jn[pl.ds(t * 4, 4)].reshape(16, D)
        return 0

    lax.fori_loop(0, 72, conv_up, 0, unroll=2)
    lax.fori_loop(0, 72, conv_dn, 0, unroll=2)
    lax.fori_loop(0, 72, conv_jn, 0, unroll=2)
    await_bytes(gain, swap_sem.at[3])

    def half(i):
        return pl.ds(pl.multiple_of(i * ROWS, ROWS), ROWS)

    def forward(i, _):
        await_bytes(hin.at[i], act_recv.at[0, i])

        @pl.when(deep)
        def _():
            joined = dot(hin[i], w_jn[...])
            await_bytes(skin.at[i], act_recv.at[1, i])
            u_s[i] = (joined + skin[i].astype(F32)).astype(BF)

        @pl.when(jnp.logical_not(deep))
        def _():
            u_s[i] = hin[i]

        values = u_s[i].astype(F32)
        center = values - jnp.mean(values, axis=-1, keepdims=True)
        inverse = lax.rsqrt(jnp.mean(center * center, axis=-1, keepdims=True) + EPSILON)
        normed = center * inverse
        normed_s[i] = normed
        inv_s[i] = jnp.broadcast_to(inverse, (ROWS, 128))
        scaled_s[half(i), :] = (normed * gain[0:1, :]).astype(BF)
        pre = dot(scaled_s[half(i), :], w_up[...])
        square = pre * pre
        bent = jnp.tanh(GELU_C * (pre + GELU_A * (square * pre)))
        grown = 0.5 * (1.0 + bent)
        active_s[half(i), :] = (pre * grown).astype(BF)
        dg_s[i] = grown + 0.5 * pre * (1.0 - bent * bent) * (GELU_C * (1.0 + 3.0 * GELU_A * square))

        @pl.when(z < 7)
        def _():
            hout[i] = (u_s[i].astype(F32) + dot(active_s[half(i), :], w_dn[...])).astype(BF)
            remote(hout.at[i], hin.at[i], act_send.at[0, i], act_recv.at[0, i], z_up).start()

        @pl.when(jnp.logical_not(deep))
        def _():
            skout[i] = dot(hout[i], w_jn[...]).astype(BF)
            remote(skout.at[i], skin.at[i], act_send.at[1, i], act_recv.at[1, i], mirror).start()
        return 0

    lax.fori_loop(0, 2, forward, 0)

    def backward(i, _):
        @pl.when(jnp.logical_not(deep))
        def _():
            await_bytes(tin.at[i], act_recv.at[3, i])
            turned = dot_nt(tin[i], w_jn[...])
            await_bytes(cin.at[i], act_recv.at[2, i])
            e_s[half(i), :] = (cin[i].astype(F32) + turned).astype(BF)

        @pl.when(deep)
        def _():
            await_bytes(cin.at[i], act_recv.at[2, i])
            e_s[half(i), :] = cin[i]

        back_in = dot_nt(e_s[half(i), :], w_dn[...])
        gp_s[half(i), :] = (dg_s[i] * back_in).astype(BF)

        @pl.when(z > 0)
        def _():
            grad_normed = dot_nt(gp_s[half(i), :], w_up[...]) * gain[0:1, :]
            normed = normed_s[i]
            first = jnp.mean(grad_normed, axis=-1, keepdims=True)
            second = jnp.mean(grad_normed * normed, axis=-1, keepdims=True)
            mixture = (grad_normed - first - normed * second) * inv_s[i][:, 0:1]
            gout[i] = (e_s[half(i), :].astype(F32) + mixture).astype(BF)

            @pl.when(deep)
            def _():
                remote(gout.at[i], tin.at[i], act_send.at[3, i], act_recv.at[3, i], mirror).start()
                cout[i] = dot_nt(gout[i], w_jn[...]).astype(BF)
                remote(cout.at[i], cin.at[i], act_send.at[2, i], act_recv.at[2, i], z_down).start()

            @pl.when(jnp.logical_not(deep))
            def _():
                remote(gout.at[i], cin.at[i], act_send.at[2, i], act_recv.at[2, i], z_down).start()
        return 0

    lax.fori_loop(0, 2, backward, 0)

    for m in range(3):
        await_bytes(gs[m].at[pl.ds(0, 135)], ag_send.at[m])
        await_bytes(gs[m].at[pl.ds(0, 144)], f_send.at[m])

    def partials(m, left, right, rows):
        def to_partner(j, _):
            t = 2 * j + 1 - c
            units = pl.ds(36 * t, 36)
            part = dot(left[pl.ds(pl.multiple_of(t * rows, rows), rows), :], right[...])
            gs[m][units] = part.reshape((36,) + UNIT[m]).astype(BF)
            remote(gs[m].at[units], rxs[m].at[pl.ds(36 * j, 36)], x_send.at[m], x_recv.at[m], partner).start()
            return 0

        def to_self(j, _):
            t = 2 * j + c
            part = dot(left[pl.ds(pl.multiple_of(t * rows, rows), rows), :], right[...])
            gs[m][pl.ds(36 * t, 36)] = part.reshape((36,) + UNIT[m]).astype(BF)
            return 0

        lax.fori_loop(0, 4, to_partner, 0)
        lax.fori_loop(0, 4, to_self, 0)

    at[...] = active_s[...].T
    partials(1, at, e_s, 288)
    lt[...] = scaled_s[...].T
    partials(0, lt, gp_s, 144)

    @pl.when(deep)
    def _():
        lt[...] = hin[...].reshape(128, D).T
        right_s[...] = gout[...].reshape(128, D)

    @pl.when(jnp.logical_not(deep))
    def _():
        lt[...] = hout[...].reshape(128, D).T
        right_s[...] = tin[...].reshape(128, D)

    partials(2, lt, right_s, 144)
    for m in range(3):
        await_bytes(rxs[m].at[...], x_recv.at[m])

    def landing(m, h, di, k):
        cnt = PART[m][h][1]
        start = (0 if h == 0 else 15 * PART[m][0][1]) + (0 if di == 0 else 8 * cnt)
        return pl.ds(start + k * cnt, cnt)

    def rs_step(k, _):
        for m in (1, 0, 2):
            for h in range(2):
                off, cnt = PART[m][h]
                for di, (d, n) in enumerate(DIRS):
                    @pl.when(k < n)
                    def _():
                        xx, yy = cycle_xy(h, rem(pos[h] + 16 - d * (n - k), 16))
                        mine = pl.ds(9 * (xx * 8 + c * 4 + yy) + off, cnt)
                        total = gs[m][mine].astype(F32) + rxs[m][pl.ds(9 * (4 * xx + yy) + off, cnt)].astype(F32)

                        @pl.when(k == 0)
                        def _():
                            gs[m][mine] = total.astype(BF)

                        @pl.when(k > 0)
                        def _():
                            before = landing(m, h, di, lax.max(k - 1, 0))
                            await_bytes(rrs[m].at[before], rs_recv.at[m, h, di, lax.max(k - 1, 0)])
                            gs[m][mine] = (total + rrs[m][before].astype(F32)).astype(BF)

                        remote(
                            gs[m].at[mine], rrs[m].at[landing(m, h, di, k)],
                            rs_send.at[m], rs_recv.at[m, h, di, k], ring[h][1 - di],
                        ).start()
        return 0

    lax.fori_loop(0, 8, rs_step, 0)
    for m in (1, 0, 2):
        for h in range(2):
            off, cnt = PART[m][h]
            mine = pl.ds(9 * own + off, cnt)
            total = gs[m][mine].astype(F32) + rxs[m][pl.ds(9 * (4 * x + y) + off, cnt)].astype(F32)
            for di, (d, n) in enumerate(DIRS):
                last = landing(m, h, di, n - 1)
                await_bytes(rrs[m].at[last], rs_recv.at[m, h, di, n - 1])
                total = total + rrs[m][last].astype(F32)
            gs[m][mine] = total.astype(BF)
        swap_copy(gs[m].at[pl.ds(9 * own, 9)], fos[m], o_send.at[m], o_recv.at[m])

    for m in (1, 0, 2):
        await_bytes(fos[m], o_recv.at[m])
        outs[m][...] = fos[m][...].astype(F32)

    for m in range(3):
        swap_sent(ins[m], swap_send.at[m])
        swap_sent(fos[m], o_send.at[m])
        await_bytes(gs[m].at[pl.ds(0, 144)], x_send.at[m])
        await_bytes(gs[m].at[pl.ds(0, 135)], rs_send.at[m])
    swap_sent(gain_in, swap_send.at[3])

    @pl.when(gives_entry)
    def _():
        for i in range(2):
            swap_sent(ent_in.at[i], io_send.at[0, i])

    @pl.when(gives_cot)
    def _():
        for i in range(2):
            swap_sent(cot_in.at[i], io_send.at[1, i])

    for i in range(2):
        @pl.when(z < 7)
        def _():
            await_bytes(hout.at[i], act_send.at[0, i])

        @pl.when(jnp.logical_not(deep))
        def _():
            await_bytes(skout.at[i], act_send.at[1, i])

        @pl.when(z > 0)
        def _():
            await_bytes(cout.at[i], act_send.at[2, i])

        @pl.when(deep)
        def _():
            await_bytes(gout.at[i], act_send.at[3, i])


def vm(*shape, dtype=BF):
    return pltpu.VMEM(shape, dtype)


def local(latents, time_table, timesteps, order, gains, w_up, w_down, w_join, cotangent):
    entry = (
        latents[order].astype(F32) + time_table[timesteps].astype(F32)[:, None, :]
    ).astype(BF)
    gain = jnp.broadcast_to(gains.astype(F32), (8, D))
    act = (2, ROWS, D)
    dma = pltpu.SemaphoreType.DMA
    scratch = (
        [vm(288, *u) for u in UNIT]
        + [vm(D, FFW), vm(FFW, D), vm(D, D)]
        + [vm(144, *u) for u in UNIT]
        + [vm(135, *u) for u in UNIT]
        + [vm(9, *u) for u in UNIT]
        + [vm(8, D, dtype=F32)]
        + [vm(*act) for _ in range(9)]
        + [
            vm(2 * ROWS, D), vm(2 * ROWS, FFW), vm(2, ROWS, FFW, dtype=F32), vm(2 * ROWS, FFW), vm(2 * ROWS, D),
            vm(*act, dtype=F32), vm(2, ROWS, 128, dtype=F32), vm(2 * ROWS, D), vm(D, 2 * ROWS), vm(FFW, 2 * ROWS),
        ]
        + [
            dma((4,)), dma((4,)), dma((2, 2)), dma((3, 2, 2, 8)), dma((3,)), dma((3,)), dma((3,)),
            dma((4, 2)), dma((4, 2)), dma((3,)), dma((3,)), dma((3, 2, 2, 8)), dma((3,)), dma((3,)), dma((3,)),
        ]
    )
    spec = pl.BlockSpec(memory_space=pltpu.VMEM)
    up, down, join = pl.pallas_call(
        kernel,
        out_shape=[jax.ShapeDtypeStruct((9,) + u, F32) for u in UNIT],
        in_specs=[spec] * 6,
        out_specs=[spec] * 3,
        scratch_shapes=scratch,
        compiler_params=pltpu.CompilerParams(
            collective_id=0, has_side_effects=True, vmem_limit_bytes=58 * 2**20
        ),
        name="blocks",
    )(
        w_up.reshape((9,) + UNIT[0]), w_down.reshape((9,) + UNIT[1]), w_join.reshape((9,) + UNIT[2]),
        gain, entry, cotangent,
    )
    return up.reshape(1, 36, FFW), down.reshape(1, 72, D), join.reshape(1, 36, D)


def solution(mesh):
    in_specs = (
        P(None, "dp", None),
        P(),
        P(),
        P(),
        P("section", None),
        P("section", "dp", None),
        P("section", "dp", None),
        P("section", "dp", None),
        P(None, "dp", None),
    )
    out_specs = (P("section", "dp", None), P("section", "dp", None), P("section", "dp", None))
    return jax.shard_map(local, mesh=mesh, in_specs=in_specs, out_specs=out_specs, check_vma=False)
```

time: 1370 us -> 260 us (0.19)
  waiting for transfers between devices: 632 us -> 0 us
  starting transfers between devices: 255 us -> 0 us
  Pallas kernels: 0 us -> 244 us
  blocking collectives: 178 us -> 0 us
  local copies, waits for them, and re-layouts: 132 us -> 11.7 us
  other arithmetic: 69 us -> 2.96 us
  matrix products: 52.7 us -> 0 us
  loops' own time: 37 us -> 0 us
  between operations: 15.4 us -> 0.67 us
    all_gather x3 -> x0, waiting for transfers between devices: 488 us -> none  [the longest x1 173 us: local(): lax.all_gather(w_up, 'dp', axis=1, tiled=True)]
    pallas_call x0 -> x1, Pallas kernels: none -> 244 us  [local(): pl.pallas_call(kernel, out_shape=[jax.ShapeDtypeStruct((9,) + u, F32) for...]
    ppermute x48 -> x0, starting transfers between devices: 208 us -> none  [the longest x30 160 us: from_partner(): return lax.ppermute(block, axis, route)]
    unnamed x1 -> x0, blocking collectives: 178 us -> none
    ppermute x48 -> x0, waiting for transfers between devices: 142 us -> none  [the longest x30 124 us: from_partner(): return lax.ppermute(block, axis, route)]
    dynamic_slice x86 -> x0, local copies, waits for them, and re-layouts: 62 us -> none  [the longest x68 51.4 us: put_slot(): current = lax.dynamic_index_in_dim(buffer, slot_index, 0, keepdims=False)]
    dot_general x15 -> x0, matrix products: 52.7 us -> none  [the longest x2 13.5 us: block_forward(): added = jnp.dot(active, down_full, preferred_element_type=jnp.float32)]
    unnamed x13 -> x0, starting transfers between devices: 46.8 us -> none
  transfers between devices with their start and end apart: 64 -> 0, of which waited for: 26 -> 0; matrix products, arithmetic and copies ran while one was open for 21% -> 0% of each run, Pallas kernels for 0% -> 0%
where the time goes in v1:
time: 260 us; the launch traced here: 259 us
  Pallas kernels  244 us (94%)
  local copies, waits for them, and re-layouts  11.7 us (4%)
  other arithmetic  2.96 us (1%)
    pallas_call x1, Pallas kernels, local(): pl.pallas_call(kernel, out_shape=[jax.ShapeDtypeStruct((9,) + u, F32) for...  244 us

profile of v1, /device:TPU:32, one launch (start us, length us, event | category | flops | bytes accessed | tf_op | source)
XLA Modules:
  0.0 259.2 jit_solution(12049574719410485562)
XLA Ops:
  0.6 0.0 copy-start
  0.6 0.8 compare_select_fusion
  1.5 0.7 compare_select_fusion.1
  2.1 0.2 copy-done
  2.3 0.6 gather_fusion.1
  2.9 0.7 convert_reduce_fusion
  3.6 0.6 broadcast_in_dim.19.gain_in
  4.2 1.6 reshape.29.jn_in
  5.8 1.6 reshape.27.up_in
  7.4 1.6 gather_fusion
  9.0 0.8 add_convert_fusion.ent_in
  9.7 243.9 %blocks.1 = (f32[9,4,2304]{2,1,0:T(4,128)}, f32[9,8,1152]{2,1,0:T(8,128)}, f32[9,4,1152]{2,1,0:T(4,128)}) custom-call(bf16[9,4,2304]{2,1,0:T(4,128)(2,1)} %reshape.27.up_in, bf16[9,8,1152]{2,1,0:T(8,128)(2,1)} %bitcast.3, bf16[9,4,1152]{2,1,0:T(4,128)(2,1)} %reshape.29.jn_in, f32[8,1152]{1,0:T(8,128)} %broadcast_in_dim.19.gain_in, ...), custom_call_target="tpu_custom_call" | custom-call | tf_op jit(solution)/shard_map/blocks/pallas_call | solution.py:427
  253.6 2.1 reshape.52
  255.7 1.8 reshape.53
  257.5 1.7 copy.17
  (3 shorter events, 0.0 us)
Async XLA Ops:
  0.6 1.7 copy-start

commit v2 on v1

v2 whole, which is shorter than its diff:
```python
import jax
import jax.numpy as jnp
from jax import lax
from jax.experimental import pallas as pl
from jax.experimental.pallas import tpu as pltpu
from jax.sharding import PartitionSpec as P

BF = jnp.bfloat16
F32 = jnp.float32
EPSILON = 1e-06
MESH = pl.DeviceIdType.MESH
D = 1152
FFW = 2304
ROWS = 32
MICROS = 4
EARLY = 2
CHUNKS = ((0, 512), (512, 640))
PART = (((0, 5, 1), (5, 4, -1)), ((0, 4, -1), (4, 5, 1)), ((0, 4, 1), (4, 5, -1)))
UNIT = ((4, FFW), (8, D), (4, D))
GELU_C = 0.7978845608028654
GELU_A = 0.044715


def rem(a, b):
    return lax.rem(a, jnp.int32(b))


def div(a, b):
    return lax.div(a, jnp.int32(b))


def dot(a, b):
    return jnp.dot(a, b, preferred_element_type=F32)


def await_bytes(ref, sem):
    pltpu.make_async_copy(ref, ref, sem).wait()


def kernel(
    up_in, dn_in, jn_in, gain_in, ent_in, cot_in,
    up_out, dn_out, jn_out,
    g_up, g_dn, g_jn, w_up, w_dn, w_jn, wt_up, wt_dn, wt_jn, rx_up, rx_dn, rx_jn, rr_up, rr_dn, rr_jn,
    st_up, st_dn, st_jn, st_gain, gain, hin, skin, cin, tin, u_s, hout, skout, cout, gout,
    scaled_s, active_s, dg_s, gp_s, e_s, mean_s, inv_s, turned_s, right_s, lt, at,
    swap_sem, swap_send, io_send, ag_recv, ag_send, f_recv, f_send,
    h_recv, h_send, c_recv, c_send, act_recv, act_send, x_recv, x_send, rs_recv, rs_send, o_recv, o_send,
):
    q = lax.axis_index("dp")
    s = lax.axis_index("section")
    x, zl, y = div(q, 8), rem(div(q, 4), 2), rem(q, 4)
    zh, c = div(s, 2), rem(s, 2)
    z = 2 * zh + zl
    deep = z >= 4

    def device(xx, yy, zz, cc):
        return (xx * 8 + rem(zz, 2) * 4 + yy, div(zz, 2) * 2 + cc)

    partner = device(x, y, z, 1 - c)
    z_up = device(x, y, rem(z + 1, 8), c)
    z_down = device(x, y, rem(z + 7, 8), c)
    mirror = device(x, y, 7 - z, c)
    swap = device(x, y, 2 * zh + c, zl)
    stays = zl == c

    def along(axis, step):
        if axis == 0:
            return device(rem(x + 4 + step, 4), y, z, c)
        return device(x, rem(y + 4 + step, 4), z, c)

    other = device(x, y, 2 * zh + 1 - zl, 1 - c)

    def owner(h, d, i, j):
        back, side = 8 - d * i, 8 - d * j
        if h == 0:
            return rem(x + side, 4), rem(y + back, 4)
        return rem(x + back, 4), rem(y + side, 4)

    gs = (g_up, g_dn, g_jn)
    rxs = (rx_up, rx_dn, rx_jn)
    rrs = (rr_up, rr_dn, rr_jn)
    outs = (up_out, dn_out, jn_out)

    def remote(src, dst, send, recv, dev):
        return pltpu.make_async_remote_copy(
            src_ref=src, dst_ref=dst, send_sem=send, recv_sem=recv, device_id=dev, device_id_type=MESH
        )

    def swap_copy(src, dst, send, recv):
        @pl.when(stays)
        def _():
            pltpu.make_async_copy(src, dst, recv).start()

        @pl.when(jnp.logical_not(stays))
        def _():
            remote(src, dst, send, recv, swap).start()

    def swap_sent(src, send):
        @pl.when(jnp.logical_not(stays))
        def _():
            await_bytes(src, send)

    ins = (st_up, st_dn, st_jn)
    st_up[...] = up_in[...].reshape((9,) + UNIT[0])
    st_dn[...] = dn_in[...].reshape((9,) + UNIT[1])
    st_jn[...] = jn_in[...].reshape((9,) + UNIT[2])
    st_gain[...] = jnp.broadcast_to(gain_in[...].astype(F32), (8, D))

    barrier = pltpu.get_barrier_semaphore()
    greet = [along(0, 1), along(0, -1), along(1, 1), along(1, -1), partner, z_up, z_down, mirror, other]
    for peer in greet:
        pl.semaphore_signal(barrier, inc=1, device_id=peer, device_id_type=MESH)
    pl.semaphore_wait(barrier, len(greet))

    for m in range(3):
        swap_copy(ins[m], gs[m].at[pl.ds(9 * q, 9)], swap_send.at[m], swap_sem.at[m])
    swap_copy(st_gain, gain, swap_send.at[3], swap_sem.at[3])
    gives_entry = (zh == 0) & (c == 0)
    gives_cot = (zh == 3) & (c == 1)

    @pl.when(gives_entry)
    def _():
        for i in range(MICROS):
            for n, (lo, size) in enumerate(CHUNKS):
                cols = pl.ds(lo, size)
                swap_copy(ent_in.at[i, :, cols], hin.at[i, :, cols], io_send.at[0, i, n], h_recv.at[i, n])

    @pl.when(gives_cot)
    def _():
        for i in range(MICROS):
            for n, (lo, size) in enumerate(CHUNKS):
                cols = pl.ds(lo, size)
                swap_copy(cot_in.at[i, :, cols], cin.at[i, :, cols], io_send.at[1, i, n], c_recv.at[i, n])

    own = x * 8 + c * 4 + y
    halves = [(m, h) for m in range(3) for h in range(2)]

    def piece(m, h, i, j):
        off, cnt, d = PART[m][h]
        xx, yy = owner(h, d, i, j)
        return gs[m].at[pl.ds(9 * (xx * 8 + c * 4 + yy) + off, cnt)]

    def spread(m, ref, axis, step, recv):
        remote(ref, ref, ag_send.at[m], recv, along(axis, step)).start()

    def to_partner(m, ref):
        remote(ref, ref, f_send.at[m], f_recv.at[m], partner).start()

    def first_axis(t, _):
        i = t + div(t, 2) * (5 - 2 * t)
        for m, h in halves:
            d = PART[m][h][2]
            f = 1 - h
            ref = piece(m, h, i, 0)

            @pl.when(i == 0)
            def _():
                if h == 0:
                    await_bytes(gs[m].at[pl.ds(9 * own, 9)], swap_sem.at[m])
                spread(m, ref, f, d, ag_recv.at[m, h, 1])
                spread(m, ref, f, -d, ag_recv.at[m, h, 3])

            @pl.when(i > 0)
            def _():
                await_bytes(ref, ag_recv.at[m, h, i])

            @pl.when(i == 1)
            def _():
                spread(m, ref, f, d, ag_recv.at[m, h, 2])

            spread(m, ref, 1 - f, d, ag_recv.at[m, h, 4 + i])
            spread(m, ref, 1 - f, -d, ag_recv.at[m, h, 12 + i])
            to_partner(m, ref)
        return 0

    def second_axis(t, _):
        i = t + div(t, 2) * (5 - 2 * t)
        for m, h in halves:
            d = PART[m][h][2]
            ref = piece(m, h, i, 1)
            await_bytes(ref, ag_recv.at[m, h, 4 + i])
            spread(m, ref, h, d, ag_recv.at[m, h, 8 + i])
            to_partner(m, ref)
            ref = piece(m, h, i, 3)
            await_bytes(ref, ag_recv.at[m, h, 12 + i])
            to_partner(m, ref)
        return 0

    def last_hop(t, _):
        i = t + div(t, 2) * (5 - 2 * t)
        for m, h in halves:
            ref = piece(m, h, i, 2)
            await_bytes(ref, ag_recv.at[m, h, 8 + i])
            to_partner(m, ref)
        return 0

    lax.fori_loop(0, 4, first_axis, 0)
    lax.fori_loop(0, 4, second_axis, 0)
    lax.fori_loop(0, 4, last_hop, 0)
    for m in range(3):
        await_bytes(gs[m].at[pl.ds(0, 144)], f_recv.at[m])

    def conv_up(t, _):
        w_up[pl.ds(pl.multiple_of(t * 16, 16), 16), :] = g_up[pl.ds(t * 4, 4)].reshape(16, FFW)
        return 0

    def conv_dn(t, _):
        w_dn[pl.ds(pl.multiple_of(t * 32, 32), 32), :] = g_dn[pl.ds(t * 4, 4)].reshape(32, D)
        return 0

    def conv_jn(t, _):
        w_jn[pl.ds(pl.multiple_of(t * 16, 16), 16), :] = g_jn[pl.ds(t * 4, 4)].reshape(16, D)
        return 0

    lax.fori_loop(0, 72, conv_up, 0, unroll=2)
    lax.fori_loop(0, 72, conv_dn, 0, unroll=2)
    lax.fori_loop(0, 72, conv_jn, 0, unroll=2)
    await_bytes(gain, swap_sem.at[3])

    def rows(i):
        return pl.ds(pl.multiple_of(i * ROWS, ROWS), ROWS)

    def transposes():
        def turn(src, dst, n):
            def one(i, _):
                block = pl.ds(pl.multiple_of(i * 128, 128), 128)
                dst[:, block] = src[block, :].T
                return 0

            lax.fori_loop(0, n, one, 0)

        turn(w_dn, wt_dn, 18)
        turn(w_up, wt_up, 9)
        turn(w_jn, wt_jn, 9)

    def forward(i, _):
        for n, (lo, size) in enumerate(CHUNKS):
            await_bytes(hin.at[i, :, pl.ds(lo, size)], h_recv.at[i, n])

        @pl.when(deep)
        def _():
            joined = dot(hin[i], w_jn[...])
            await_bytes(skin.at[i], act_recv.at[0, i])
            u_s[i] = (joined + skin[i].astype(F32)).astype(BF)

        @pl.when(jnp.logical_not(deep))
        def _():
            u_s[i] = hin[i]

        values = u_s[i].astype(F32)
        middle = jnp.mean(values, axis=-1, keepdims=True)
        center = values - middle
        inverse = lax.rsqrt(jnp.mean(center * center, axis=-1, keepdims=True) + EPSILON)
        normed = center * inverse
        mean_s[i] = jnp.broadcast_to(middle, (ROWS, 128))
        inv_s[i] = jnp.broadcast_to(inverse, (ROWS, 128))
        scaled_s[rows(i), :] = (normed * gain[0:1, :]).astype(BF)
        pre = dot(scaled_s[rows(i), :], w_up[...])
        square = pre * pre
        bent = jnp.tanh(GELU_C * (pre + GELU_A * (square * pre)))
        grown = 0.5 * (1.0 + bent)
        active_s[rows(i), :] = (pre * grown).astype(BF)
        dg_s[i] = grown + 0.5 * pre * (1.0 - bent * bent) * (GELU_C * (1.0 + 3.0 * GELU_A * square))

        @pl.when(z < 7)
        def _():
            for n, (lo, size) in enumerate(CHUNKS):
                cols = pl.ds(lo, size)
                grown_by = dot(active_s[rows(i), :], w_dn[:, cols])
                hout[i, :, cols] = (u_s[i, :, cols].astype(F32) + grown_by).astype(BF)
                remote(hout.at[i, :, cols], hin.at[i, :, cols], h_send.at[i, n], h_recv.at[i, n], z_up).start()

        @pl.when(jnp.logical_not(deep))
        def _():
            skout[i] = dot(hout[i], w_jn[...]).astype(BF)
            remote(skout.at[i], skin.at[i], act_send.at[0, i], act_recv.at[0, i], mirror).start()
        return 0

    @pl.when(deep)
    def _():
        transposes()

    lax.fori_loop(0, MICROS, forward, 0)

    @pl.when(jnp.logical_not(deep))
    def _():
        transposes()

    for m in range(3):
        await_bytes(gs[m].at[pl.ds(0, 135)], ag_send.at[m])
        await_bytes(gs[m].at[pl.ds(0, 144)], f_send.at[m])

    def partials(m, left, right, size, to_partner):
        def one(j, _):
            t = 2 * j + (1 - c if to_partner else c)
            units = pl.ds(36 * t, 36)
            part = dot(left[pl.ds(pl.multiple_of(t * size, size), size), :], right[...])
            gs[m][units] = part.reshape((36,) + UNIT[m]).astype(BF)
            if to_partner:
                remote(gs[m].at[units], rxs[m].at[pl.ds(36 * j, 36)], x_send.at[m], x_recv.at[m], partner).start()
            return 0

        lax.fori_loop(0, 4, one, 0)

    def join_partials():
        @pl.when(deep)
        def _():
            lt[...] = hin[...].reshape(128, D).T
            right_s[...] = gout[...].reshape(128, D)

        @pl.when(jnp.logical_not(deep))
        def _():
            lt[...] = hout[...].reshape(128, D).T
            right_s[...] = tin[...].reshape(128, D)

        partials(2, lt, right_s, 144, True)
        partials(2, lt, right_s, 144, False)

    def reduce_scatter(which):
        parts = [(m, h) for m in which for h in range(2)]
        for m in which:
            await_bytes(rxs[m].at[...], x_recv.at[m])

        def rows_of(m, h, i, j):
            off, cnt, d = PART[m][h]
            xx, yy = owner(h, d, i, j)
            return pl.ds(9 * (xx * 8 + c * 4 + yy) + off, cnt), pl.ds(9 * (4 * xx + yy) + off, cnt)

        def landing(m, h, n):
            cnt = PART[m][h][1]
            return pl.ds((0 if h == 0 else 15 * PART[m][0][1]) + n * cnt, cnt)

        def arrived(m, h, n):
            spot = landing(m, h, n)
            await_bytes(rrs[m].at[spot], rs_recv.at[m, h, n])
            return rrs[m][spot].astype(F32)

        def settle(m, h, i, j, slots):
            mine, theirs = rows_of(m, h, i, j)
            total = gs[m][mine].astype(F32) + rxs[m][theirs].astype(F32)
            for n in slots:
                total = total + arrived(m, h, n)
            gs[m][mine] = total.astype(BF)
            return gs[m].at[mine]

        def send(m, h, ref, axis, step, n):
            remote(
                ref, rrs[m].at[landing(m, h, n)], rs_send.at[m], rs_recv.at[m, h, n], along(axis, step)
            ).start()

        def far(i, _):
            for m, h in parts:
                send(m, h, settle(m, h, i, 2, ()), h, -PART[m][h][2], i)
            return 0

        def near(i, _):
            for m, h in parts:
                send(m, h, settle(m, h, i, 3, ()), h, PART[m][h][2], 4 + i)
            return 0

        def middle(i, _):
            for m, h in parts:
                send(m, h, settle(m, h, i, 1, (i,)), h, -PART[m][h][2], 8 + i)
            return 0

        lax.fori_loop(0, 4, far, 0)
        lax.fori_loop(0, 4, near, 0)
        lax.fori_loop(0, 4, middle, 0)
        for m, h in parts:
            send(m, h, settle(m, h, 2, 0, (6, 10)), 1 - h, -PART[m][h][2], 12)
        for m, h in parts:
            send(m, h, settle(m, h, 3, 0, (7, 11)), 1 - h, PART[m][h][2], 14)
        for m, h in parts:
            send(m, h, settle(m, h, 1, 0, (5, 9, 12)), 1 - h, -PART[m][h][2], 13)
        for m, h in parts:
            settle(m, h, 0, 0, (4, 8, 13, 14))
            if h == 1:
                swap_copy(gs[m].at[pl.ds(9 * own, 9)], outs[m], o_send.at[m], o_recv.at[m])

    @pl.when(z <= EARLY)
    def _():
        for i in range(MICROS):
            await_bytes(tin.at[i], act_recv.at[1, i])
        turned_s[...] = dot(tin[...].reshape(128, D), wt_jn[...]).reshape(MICROS, ROWS, D)
        join_partials()

    @pl.when(z == 0)
    def _():
        reduce_scatter((2,))

    def backward(i, _):
        @pl.when(deep)
        def _():
            for n, (lo, size) in enumerate(CHUNKS):
                await_bytes(cin.at[i, :, pl.ds(lo, size)], c_recv.at[i, n])
            e_s[rows(i), :] = cin[i]

        @pl.when(jnp.logical_not(deep))
        def _():
            @pl.when(z > EARLY)
            def _():
                await_bytes(tin.at[i], act_recv.at[1, i])
                turned_s[i] = dot(tin[i], wt_jn[...])

            for n, (lo, size) in enumerate(CHUNKS):
                await_bytes(cin.at[i, :, pl.ds(lo, size)], c_recv.at[i, n])
            e_s[rows(i), :] = (cin[i].astype(F32) + turned_s[i]).astype(BF)

        back_in = dot(e_s[rows(i), :], wt_dn[...])
        gp_s[rows(i), :] = (dg_s[i] * back_in).astype(BF)

        @pl.when(z > 0)
        def _():
            grad_normed = dot(gp_s[rows(i), :], wt_up[...]) * gain[0:1, :]
            inverse = inv_s[i][:, 0:1]
            normed = (u_s[i].astype(F32) - mean_s[i][:, 0:1]) * inverse
            first = jnp.mean(grad_normed, axis=-1, keepdims=True)
            second = jnp.mean(grad_normed * normed, axis=-1, keepdims=True)
            mixture = (grad_normed - first - normed * second) * inverse
            gout[i] = (e_s[rows(i), :].astype(F32) + mixture).astype(BF)

            @pl.when(deep)
            def _():
                remote(gout.at[i], tin.at[i], act_send.at[1, i], act_recv.at[1, i], mirror).start()
                for n, (lo, size) in enumerate(CHUNKS):
                    cols = pl.ds(lo, size)
                    cout[i, :, cols] = dot(gout[i], wt_jn[:, cols]).astype(BF)
                    remote(cout.at[i, :, cols], cin.at[i, :, cols], c_send.at[i, n], c_recv.at[i, n], z_down).start()

            @pl.when(jnp.logical_not(deep))
            def _():
                for n, (lo, size) in enumerate(CHUNKS):
                    cols = pl.ds(lo, size)
                    remote(gout.at[i, :, cols], cin.at[i, :, cols], c_send.at[i, n], c_recv.at[i, n], z_down).start()
        return 0

    lax.fori_loop(0, MICROS, backward, 0)

    at[...] = active_s[...].T
    partials(1, at, e_s, 288, True)
    lt[...] = scaled_s[...].T
    partials(0, lt, gp_s, 144, True)
    partials(1, at, e_s, 288, False)
    partials(0, lt, gp_s, 144, False)

    @pl.when(z > EARLY)
    def _():
        join_partials()

    @pl.when(z == 0)
    def _():
        reduce_scatter((1, 0))

    @pl.when(z > 0)
    def _():
        reduce_scatter((1, 0, 2))

    for m in (2, 1, 0):
        await_bytes(outs[m], o_recv.at[m])

    for m in range(3):
        swap_sent(ins[m], swap_send.at[m])
        swap_sent(outs[m], o_send.at[m])
        await_bytes(gs[m].at[pl.ds(0, 144)], x_send.at[m])
        await_bytes(gs[m].at[pl.ds(0, 135)], rs_send.at[m])
    swap_sent(st_gain, swap_send.at[3])

    for i in range(MICROS):
        for n, (lo, size) in enumerate(CHUNKS):
            piece = hout.at[i, :, pl.ds(lo, size)]

            @pl.when(gives_entry)
            def _():
                swap_sent(piece, io_send.at[0, i, n])

            @pl.when(gives_cot)
            def _():
                swap_sent(piece, io_send.at[1, i, n])

            @pl.when(z < 7)
            def _():
                await_bytes(piece, h_send.at[i, n])

            @pl.when(z > 0)
            def _():
                await_bytes(piece, c_send.at[i, n])

        @pl.when(jnp.logical_not(deep))
        def _():
            await_bytes(skout.at[i], act_send.at[0, i])

        @pl.when(deep)
        def _():
            await_bytes(gout.at[i], act_send.at[1, i])


def pick(steps, order, lat, table, out):
    row = rem(steps[pl.program_id(0)], 16)
    here = lax.broadcasted_iota(jnp.int32, (16, D), 0) == row
    moved = jnp.sum(jnp.where(here, table[...].astype(F32), 0.0), axis=0, keepdims=True)
    out[0] = (lat[0].astype(F32) + moved).astype(BF)


def widen(up, dn, jn, up_out, dn_out, jn_out):
    up_out[...] = up[...].astype(F32).reshape(up_out.shape)
    dn_out[...] = dn[...].astype(F32).reshape(dn_out.shape)
    jn_out[...] = jn[...].astype(F32).reshape(jn_out.shape)


def vm(*shape, dtype=BF):
    return pltpu.VMEM(shape, dtype)


def local(latents, time_table, timesteps, order, gains, w_up, w_down, w_join, cotangent):
    act = (MICROS, ROWS, D)
    tokens = MICROS * ROWS
    chunks = len(CHUNKS)
    dma = pltpu.SemaphoreType.DMA
    full = [vm(D, FFW), vm(FFW, D), vm(D, D)]
    scratch = (
        [vm(288, *u) for u in UNIT]
        + full
        + [vm(FFW, D), vm(D, FFW), vm(D, D)]
        + [vm(144, *u) for u in UNIT]
        + [vm(135, *u) for u in UNIT]
        + [vm(9, *u) for u in UNIT]
        + [vm(8, D, dtype=F32), vm(8, D, dtype=F32)]
        + [vm(*act) for _ in range(9)]
        + [
            vm(tokens, D), vm(tokens, FFW), vm(MICROS, ROWS, FFW, dtype=F32), vm(tokens, FFW), vm(tokens, D),
            vm(MICROS, ROWS, 128, dtype=F32), vm(MICROS, ROWS, 128, dtype=F32), vm(*act, dtype=F32),
            vm(tokens, D), vm(D, tokens), vm(FFW, tokens),
        ]
        + [
            dma((4,)), dma((4,)), dma((2, MICROS, chunks)), dma((3, 2, 16)), dma((3,)), dma((3,)), dma((3,)),
            dma((MICROS, chunks)), dma((MICROS, chunks)), dma((MICROS, chunks)), dma((MICROS, chunks)),
            dma((2, MICROS)), dma((2, MICROS)), dma((3,)), dma((3,)),
            dma((3, 2, 15)), dma((3,)), dma((3,)), dma((3,)),
        ]
    )
    spec = pl.BlockSpec(memory_space=pltpu.VMEM)
    micros, images, _ = latents.shape
    entry = pl.pallas_call(
        pick,
        grid_spec=pltpu.PrefetchScalarGridSpec(
            num_scalar_prefetch=2,
            grid=(micros,),
            in_specs=[
                pl.BlockSpec((1, images, D), lambda m, steps, order: (order[m], 0, 0)),
                pl.BlockSpec((16, D), lambda m, steps, order: (div(steps[m], 16), 0)),
            ],
            out_specs=pl.BlockSpec((1, images, D), lambda m, steps, order: (m, 0, 0)),
        ),
        out_shape=jax.ShapeDtypeStruct(latents.shape, BF),
        name="entries",
    )(timesteps, order, latents, time_table)
    sums = pl.pallas_call(
        kernel,
        out_shape=[jax.ShapeDtypeStruct((9,) + u, BF) for u in UNIT],
        in_specs=[spec] * 6,
        out_specs=[spec] * 3,
        scratch_shapes=scratch,
        compiler_params=pltpu.CompilerParams(
            collective_id=0, has_side_effects=True, vmem_limit_bytes=63 * 2**20
        ),
        name="blocks",
    )(w_up[0], w_down[0], w_join[0], gains, entry.reshape(act), cotangent.reshape(act))
    up, down, join = pl.pallas_call(
        widen,
        out_shape=[
            jax.ShapeDtypeStruct((36, 1, FFW), F32),
            jax.ShapeDtypeStruct((72, D), F32),
            jax.ShapeDtypeStruct((36, 1, D), F32),
        ],
        in_specs=[spec] * 3,
        out_specs=[spec] * 3,
        name="widen",
    )(*sums)
    return jnp.swapaxes(up, 0, 1), down[None], jnp.swapaxes(join, 0, 1)


def solution(mesh):
    in_specs = (
        P(None, "dp", None),
        P(),
        P(),
        P(),
        P("section", None),
        P("section", "dp", None),
        P("section", "dp", None),
        P("section", "dp", None),
        P(None, "dp", None),
    )
    out_specs = (P("section", "dp", None), P("section", "dp", None), P("section", "dp", None))
    return jax.shard_map(local, mesh=mesh, in_specs=in_specs, out_specs=out_specs, check_vma=False)
```

time: 260 us -> 212 us (0.82); the launches traced: 259 us -> 208 us
  Pallas kernels: 244 us -> 208 us
  local copies, waits for them, and re-layouts: 11.7 us -> 0 us
  other arithmetic: 2.96 us -> 0 us
    pallas_call x1 -> x3, Pallas kernels: 244 us -> 208 us  [the longest x1 203 us: local(): pl.pallas_call(kernel, out_shape=[jax.ShapeDtypeStruct((9,) + u, BF) for...]
    reshape x4 -> x0, local copies, waits for them, and re-layouts: 7.08 us -> none  [the longest x1 2.1 us: local(): up.reshape(1, 36, FFW)]
where the time goes in v2:
time: 212 us; the launch traced here: 208 us
  Pallas kernels  208 us (98%)
    pallas_call x1, Pallas kernels, local(): pl.pallas_call(kernel, out_shape=[jax.ShapeDtypeStruct((9,) + u, BF) for...  203 us

profile of v2, /device:TPU:32, one launch (start us, length us, event | category | flops | bytes accessed | tf_op | source)
XLA Modules:
  0.0 208.4 jit_solution(17953695337122681228)
XLA Ops:
  0.6 2.4 %entries.1 = bf16[2,64,1152]{2,1,0:T(8,128)(2,1)} custom-call(s32[2]{0:T(128)} %steps.1, s32[2]{0:T(128)} %order.1, bf16[2,64,1152]{2,1,0:T(8,128)(2,1)} %lat.1, bf16[1000,1152]{1,0:T(8,128)(2,1)} %table.1), custom_call_target="tpu_custom_call" | custom-call | tf_op jit(solution)/shard_map/entries/pallas_call | solution.py:543
  3.0 203.4 %blocks.1 = (bf16[9,4,2304]{2,1,0:T(4,128)(2,1)}, bf16[9,8,1152]{2,1,0:T(8,128)(2,1)}, bf16[9,4,1152]{2,1,0:T(4,128)(2,1)}) custom-call(bf16[36,2304]{1,0:T(8,128)(2,1)} %bitcast.10, bf16[72,1152]{1,0:T(8,128)(2,1)} %bitcast.11, bf16[36,1152]{1,0:T(8,128)(2,1)} %bitcast.12, bf16[1,1152]{1,0:T(2,128)(2,1)} %gain_in.1, bf16[4,32,1152]{2,1,0:T(8,128)(2,1)} %bitcast.8, ...), custom_call_target="tpu_custom_call" | custom-call | tf_op jit(solution)/shard_map/blocks/pallas_call | solution.py:557
  206.4 2.0 widen.1

commit v3 on v2

v3 whole, which is shorter than its diff:
```python
import jax
import jax.numpy as jnp
from jax import lax
from jax.experimental import pallas as pl
from jax.experimental.pallas import tpu as pltpu
from jax.sharding import PartitionSpec as P

BF = jnp.bfloat16
F32 = jnp.float32
EPSILON = 1e-06
MESH = pl.DeviceIdType.MESH
D = 1152
FFW = 2304
ROWS = 32
GROUPS = 8
FEWER, MICROS = 3, 5
EARLY = 2
CHUNKS = ((0, 512), (512, 640))
PART = (((0, 5, 1), (5, 4, -1)), ((0, 4, -1), (4, 5, 1)), ((0, 4, 1), (4, 5, -1)))
UNIT = ((4, FFW), (8, D), (4, D))
GELU_C = 0.7978845608028654
GELU_A = 0.044715


def rem(a, b):
    return lax.rem(a, jnp.int32(b))


def div(a, b):
    return lax.div(a, jnp.int32(b))


def dot(a, b):
    return jnp.dot(a, b, preferred_element_type=F32)


def await_bytes(ref, sem):
    pltpu.make_async_copy(ref, ref, sem).wait()


def kernel(
    steps, order, up_in, dn_in, jn_in, gain_in, lat_in, time_in, cot_in,
    up_out, dn_out, jn_out,
    g_up, g_dn, g_jn, w_up, w_dn, w_jn, wt_up, wt_dn, wt_jn, rr_up, rr_dn, rr_jn,
    st_up, st_dn, st_jn, st_gain, gain, hin, skin, cin, tin, u_s, hout, skout, cout, gout,
    dg_s, mean_s, inv_s, turned_s, scaled_g, active_g, e_g, gp_g, left_g, right_g, scaled_t, active_t,
    time_sem, swap_sem, swap_send, io_send, ag_recv, ag_send, f_recv, f_send,
    h_recv, h_send, c_recv, c_send, act_recv, act_send, x_recv, x_send, rs_recv, rs_send, o_recv, o_send,
):
    q = lax.axis_index("dp")
    s = lax.axis_index("section")
    x, zl, y = div(q, 8), rem(div(q, 4), 2), rem(q, 4)
    zh, c = div(s, 2), rem(s, 2)
    z = 2 * zh + zl
    deep = z >= 4
    first, count = MICROS * (1 - c), FEWER + (MICROS - FEWER) * c
    first_there, count_there = MICROS * c, MICROS - (MICROS - FEWER) * c

    def device(xx, yy, zz, cc):
        return (xx * 8 + rem(zz, 2) * 4 + yy, div(zz, 2) * 2 + cc)

    partner = device(x, y, z, 1 - c)
    z_up = device(x, y, rem(z + 1, 8), c)
    z_down = device(x, y, rem(z + 7, 8), c)
    mirror = device(x, y, 7 - z, c)
    swap = device(x, y, 2 * zh + c, zl)
    stays = zl == c

    def along(axis, step):
        if axis == 0:
            return device(rem(x + 4 + step, 4), y, z, c)
        return device(x, rem(y + 4 + step, 4), z, c)

    other = device(x, y, 2 * zh + 1 - zl, 1 - c)

    def owner(h, d, i, j):
        back, side = 8 - d * i, 8 - d * j
        if h == 0:
            return rem(x + side, 4), rem(y + back, 4)
        return rem(x + back, 4), rem(y + side, 4)

    gs = (g_up, g_dn, g_jn)
    shared = (scaled_g, active_g, e_g, gp_g, left_g, right_g)
    rrs = (rr_up, rr_dn, rr_jn)
    outs = (up_out, dn_out, jn_out)

    def remote(src, dst, send, recv, dev):
        return pltpu.make_async_remote_copy(
            src_ref=src, dst_ref=dst, send_sem=send, recv_sem=recv, device_id=dev, device_id_type=MESH
        )

    def swap_copy(src, dst, send, recv):
        @pl.when(stays)
        def _():
            pltpu.make_async_copy(src, dst, recv).start()

        @pl.when(jnp.logical_not(stays))
        def _():
            remote(src, dst, send, recv, swap).start()

    def swap_sent(src, send):
        @pl.when(jnp.logical_not(stays))
        def _():
            await_bytes(src, send)

    ins = (st_up, st_dn, st_jn)
    st_up[...] = up_in[...].reshape((9,) + UNIT[0])
    st_dn[...] = dn_in[...].reshape((9,) + UNIT[1])
    st_jn[...] = jn_in[...].reshape((9,) + UNIT[2])
    st_gain[...] = jnp.broadcast_to(gain_in[...].astype(F32), (8, D))

    barrier = pltpu.get_barrier_semaphore()
    greet = [along(0, 1), along(0, -1), along(1, 1), along(1, -1), partner, z_up, z_down, mirror, other]
    for peer in greet:
        pl.semaphore_signal(barrier, inc=1, device_id=peer, device_id_type=MESH)
    pl.semaphore_wait(barrier, len(greet))

    for m in range(3):
        swap_copy(ins[m], gs[m].at[pl.ds(9 * q, 9)], swap_send.at[m], swap_sem.at[m])
    swap_copy(st_gain, gain, swap_send.at[3], swap_sem.at[3])
    gives_entry = (zh == 0) & (c == 0)
    gives_cot = (zh == 3) & (c == 1)

    def hand_in(src, dst, send, recv):
        for i in range(4):
            for n, (lo, size) in enumerate(CHUNKS):
                cols = pl.ds(lo, size)
                if i < FEWER:
                    swap_copy(src.at[i, :, cols], dst.at[i, :, cols], send.at[i, n], recv.at[i, n])
                    continue

                @pl.when(zl == 1)
                def _():
                    swap_copy(src.at[i, :, cols], dst.at[i, :, cols], send.at[i, n], recv.at[i, n])

                @pl.when(zl == 0)
                def _():
                    remote(
                        src.at[i, :, cols], dst.at[i - FEWER + 4, :, cols], send.at[i, n], recv.at[i - FEWER + 4, n],
                        device(x, y, 2 * zh + c, 1),
                    ).start()

    @pl.when(gives_entry)
    def _():
        table = rr_dn.at[pl.ds(0, time_in.shape[0])]
        pltpu.make_async_copy(time_in, table, time_sem).start()
        await_bytes(table, time_sem)
        row = lax.broadcasted_iota(jnp.int32, (8, D), 0)
        for m in range(2):
            block = rr_dn[div(steps[m], 8)].astype(F32)
            shift = jnp.sum(jnp.where(row == rem(steps[m], 8), block, 0.0), axis=0, keepdims=True)
            moved = lat_in[order[m]].astype(F32) + shift
            gout[2 * m:2 * m + 2] = moved.astype(BF).reshape(2, ROWS, D)
        hand_in(gout, hin, io_send.at[0], h_recv)

    @pl.when(gives_cot)
    def _():
        hand_in(cot_in, cin, io_send.at[1], c_recv)

    own = x * 8 + c * 4 + y

    def piece(m, h, i, j):
        off, cnt, d = PART[m][h]
        xx, yy = owner(h, d, i, j)
        return gs[m].at[pl.ds(9 * (xx * 8 + c * 4 + yy) + off, cnt)]

    def spread(m, ref, axis, step, recv):
        remote(ref, ref, ag_send.at[m], recv, along(axis, step)).start()

    def to_partner(m, ref):
        remote(ref, ref, f_send.at[m], f_recv.at[m], partner).start()

    def legs(weight):
        parts = [(weight, h) for h in range(2)]

        def first_axis(t, _):
            i = t + div(t, 2) * (5 - 2 * t)
            for m, h in parts:
                d = PART[m][h][2]
                f = 1 - h
                ref = piece(m, h, i, 0)

                @pl.when(i == 0)
                def _():
                    if h == 0:
                        await_bytes(gs[m].at[pl.ds(9 * own, 9)], swap_sem.at[m])
                    spread(m, ref, f, d, ag_recv.at[m, h, 1])
                    spread(m, ref, f, -d, ag_recv.at[m, h, 3])

                @pl.when(i > 0)
                def _():
                    await_bytes(ref, ag_recv.at[m, h, i])

                @pl.when(i == 1)
                def _():
                    spread(m, ref, f, d, ag_recv.at[m, h, 2])

                spread(m, ref, 1 - f, d, ag_recv.at[m, h, 4 + i])
                spread(m, ref, 1 - f, -d, ag_recv.at[m, h, 12 + i])
                to_partner(m, ref)
            return 0

        def second_axis(t, _):
            i = t + div(t, 2) * (5 - 2 * t)
            for m, h in parts:
                d = PART[m][h][2]
                ref = piece(m, h, i, 1)
                await_bytes(ref, ag_recv.at[m, h, 4 + i])
                spread(m, ref, h, d, ag_recv.at[m, h, 8 + i])
                to_partner(m, ref)
                ref = piece(m, h, i, 3)
                await_bytes(ref, ag_recv.at[m, h, 12 + i])
                to_partner(m, ref)
            return 0

        def last_hop(t, _):
            i = t + div(t, 2) * (5 - 2 * t)
            for m, h in parts:
                ref = piece(m, h, i, 2)
                await_bytes(ref, ag_recv.at[m, h, 8 + i])
                to_partner(m, ref)
            return 0

        return first_axis, second_axis, last_hop

    def conv(m):
        src, dst = gs[m], (w_up, w_dn, w_jn)[m]
        size = 4 * UNIT[m][0]

        def one(t, _):
            block = src[pl.ds(t * 4, 4)].reshape(size, UNIT[m][1])
            dst[pl.ds(pl.multiple_of(t * size, size), size), :] = block
            return 0

        lax.fori_loop(0, 72, one, 0, unroll=2)

    def gather(which):
        walks = [legs(m) for m in which]
        for leg in range(3):
            def all_of(t, _):
                for walk in walks:
                    walk[leg](t, 0)
                return 0

            lax.fori_loop(0, 4, all_of, 0)
        for m in which:
            await_bytes(gs[m].at[pl.ds(0, 144)], f_recv.at[m])
            conv(m)

    @pl.when(z <= 1)
    def _():
        gather((0, 1))

    @pl.when(z > 1)
    def _():
        gather((0, 1, 2))

    await_bytes(gain, swap_sem.at[3])

    def rows(i):
        return pl.ds(pl.multiple_of(i * ROWS, ROWS), ROWS)

    def transposes():
        def turn(src, dst, n):
            def one(i, _):
                block = pl.ds(pl.multiple_of(i * 128, 128), 128)
                dst[:, block] = src[block, :].T
                return 0

            lax.fori_loop(0, n, one, 0)

        turn(w_dn, wt_dn, 18)
        turn(w_up, wt_up, 9)
        turn(w_jn, wt_jn, 9)

    def show(kind, i):
        ref = shared[kind].at[rows(first + i)]
        remote(ref, ref, x_send.at[kind, first + i], x_recv.at[kind, first + i], partner).start()

    def seen(kind):
        def one(i, _):
            await_bytes(shared[kind].at[rows(first_there + i)], x_recv.at[kind, first_there + i])
            return 0

        lax.fori_loop(0, count_there, one, 0)

    def give_skip(i):
        skout[i] = dot(hout[i], w_jn[...]).astype(BF)
        remote(skout.at[i], skin.at[i], act_send.at[0, i], act_recv.at[0, i], mirror).start()

    def forward(i, _):
        mine = rows(first + i)
        for n, (lo, size) in enumerate(CHUNKS):
            await_bytes(hin.at[i, :, pl.ds(lo, size)], h_recv.at[i, n])

        @pl.when(deep)
        def _():
            joined = dot(hin[i], w_jn[...])
            await_bytes(skin.at[i], act_recv.at[0, i])
            u_s[i] = (joined + skin[i].astype(F32)).astype(BF)

        @pl.when(jnp.logical_not(deep))
        def _():
            u_s[i] = hin[i]

        values = u_s[i].astype(F32)
        middle = jnp.mean(values, axis=-1, keepdims=True)
        center = values - middle
        inverse = lax.rsqrt(jnp.mean(center * center, axis=-1, keepdims=True) + EPSILON)
        normed = center * inverse
        mean_s[i] = jnp.broadcast_to(middle, (ROWS, 128))
        inv_s[i] = jnp.broadcast_to(inverse, (ROWS, 128))
        scaled_g[mine, :] = (normed * gain[0:1, :]).astype(BF)
        pre = dot(scaled_g[mine, :], w_up[...])
        square = pre * pre
        bent = jnp.tanh(GELU_C * (pre + GELU_A * (square * pre)))
        grown = 0.5 * (1.0 + bent)
        active_g[mine, :] = (pre * grown).astype(BF)
        dg_s[i] = grown + 0.5 * pre * (1.0 - bent * bent) * (GELU_C * (1.0 + 3.0 * GELU_A * square))

        @pl.when(z < 7)
        def _():
            for n, (lo, size) in enumerate(CHUNKS):
                cols = pl.ds(lo, size)
                grown_by = dot(active_g[mine, :], w_dn[:, cols])
                hout[i, :, cols] = (u_s[i, :, cols].astype(F32) + grown_by).astype(BF)
                remote(hout.at[i, :, cols], hin.at[i, :, cols], h_send.at[i, n], h_recv.at[i, n], z_up).start()

        @pl.when(deep)
        def _():
            left_g[mine, :] = hin[i]

        @pl.when(jnp.logical_not(deep))
        def _():
            @pl.when(z > EARLY)
            def _():
                give_skip(i)

            left_g[mine, :] = hout[i]

        show(0, i)
        show(1, i)
        show(4, i)
        return 0

    for i in range(4):
        for n, (lo, size) in enumerate(CHUNKS):
            part = hout.at[i, :, pl.ds(lo, size)]
            for gives, kind in ((gives_entry, 0), (gives_cot, 1)):
                @pl.when(gives)
                def _():
                    if i < FEWER:
                        swap_sent(part, io_send.at[kind, i, n])
                        return

                    @pl.when(zl == 1)
                    def _():
                        swap_sent(part, io_send.at[kind, i, n])

                    @pl.when(zl == 0)
                    def _():
                        await_bytes(part, io_send.at[kind, i, n])

    @pl.when(deep)
    def _():
        transposes()

    lax.fori_loop(0, count, forward, 0)

    @pl.when(z <= 1)
    def _():
        gather((2,))

    @pl.when(z <= EARLY)
    def _():
        def one(i, _):
            give_skip(i)
            return 0

        lax.fori_loop(0, count, one, 0)

    @pl.when(jnp.logical_not(deep))
    def _():
        transposes()

    for m in range(3):
        await_bytes(gs[m].at[pl.ds(0, 135)], ag_send.at[m])
        await_bytes(gs[m].at[pl.ds(0, 144)], f_send.at[m])

    def partials(m, left, right, size):
        def one(j, _):
            t = 2 * j + c
            part = dot(left[pl.ds(pl.multiple_of(t * size, size), size), :], right[...])
            gs[m][pl.ds(36 * t, 36)] = part.reshape((36,) + UNIT[m]).astype(BF)
            return 0

        lax.fori_loop(0, 4, one, 0)

    def turn_activations():
        seen(0)
        seen(1)
        scaled_t[...] = scaled_g[...].T
        active_t[...] = active_g[...].T

    def join_partials():
        seen(4)
        seen(5)
        scaled_t[...] = left_g[...].T
        partials(2, scaled_t, right_g, 144)

    def piece_rows(m, h, i, j):
        off, cnt, d = PART[m][h]
        xx, yy = owner(h, d, i, j)
        return pl.ds(9 * (xx * 8 + c * 4 + yy) + off, cnt)

    def landing(m, h, n):
        cnt = PART[m][h][1]
        return pl.ds((0 if h == 0 else 15 * PART[m][0][1]) + n * cnt, cnt)

    def pass_on(m, h, mine, axis, step, n):
        remote(
            gs[m].at[mine], rrs[m].at[landing(m, h, n)], rs_send.at[m], rs_recv.at[m, h, n], along(axis, step)
        ).start()

    def launch(m):
        def one(i, _):
            for h in range(2):
                d = PART[m][h][2]
                pass_on(m, h, piece_rows(m, h, i, 2), h, -d, i)
                pass_on(m, h, piece_rows(m, h, i, 3), h, d, 4 + i)
            return 0

        lax.fori_loop(0, 4, one, 0)

    def collect(which):
        parts = [(m, h) for m in which for h in range(2)]

        def settle(m, h, i, j, slots):
            mine = piece_rows(m, h, i, j)
            total = gs[m][mine].astype(F32)
            for n in slots:
                spot = landing(m, h, n)
                await_bytes(rrs[m].at[spot], rs_recv.at[m, h, n])
                total = total + rrs[m][spot].astype(F32)
            gs[m][mine] = total.astype(BF)
            return mine

        def middle(i, _):
            for m, h in parts:
                pass_on(m, h, settle(m, h, i, 1, (i,)), h, -PART[m][h][2], 8 + i)
            return 0

        lax.fori_loop(0, 4, middle, 0)
        for m, h in parts:
            pass_on(m, h, settle(m, h, 2, 0, (6, 10)), 1 - h, -PART[m][h][2], 12)
        for m, h in parts:
            pass_on(m, h, settle(m, h, 3, 0, (7, 11)), 1 - h, PART[m][h][2], 14)
        for m, h in parts:
            pass_on(m, h, settle(m, h, 1, 0, (5, 9, 12)), 1 - h, -PART[m][h][2], 13)
        for m, h in parts:
            settle(m, h, 0, 0, (4, 8, 13, 14))
            if h == 1:
                swap_copy(gs[m].at[pl.ds(9 * own, 9)], outs[m], o_send.at[m], o_recv.at[m])

    @pl.when(z <= EARLY)
    def _():
        def one(i, _):
            await_bytes(tin.at[i], act_recv.at[1, i])
            right_g[rows(first + i), :] = tin[i]
            show(5, i)
            turned_s[i] = dot(tin[i], wt_jn[...])
            return 0

        lax.fori_loop(0, count, one, 0)
        join_partials()
        launch(2)
        turn_activations()

    @pl.when(z == 0)
    def _():
        collect((2,))

    def backward(i, _):
        mine = rows(first + i)

        @pl.when(deep)
        def _():
            for n, (lo, size) in enumerate(CHUNKS):
                await_bytes(cin.at[i, :, pl.ds(lo, size)], c_recv.at[i, n])
            e_g[mine, :] = cin[i]

        @pl.when(jnp.logical_not(deep))
        def _():
            @pl.when(z > EARLY)
            def _():
                await_bytes(tin.at[i], act_recv.at[1, i])
                right_g[mine, :] = tin[i]
                turned_s[i] = dot(tin[i], wt_jn[...])

            for n, (lo, size) in enumerate(CHUNKS):
                await_bytes(cin.at[i, :, pl.ds(lo, size)], c_recv.at[i, n])
            e_g[mine, :] = (cin[i].astype(F32) + turned_s[i]).astype(BF)

        back_in = dot(e_g[mine, :], wt_dn[...])
        gp_g[mine, :] = (dg_s[i] * back_in).astype(BF)

        @pl.when(z > 0)
        def _():
            grad_normed = dot(gp_g[mine, :], wt_up[...]) * gain[0:1, :]
            inverse = inv_s[i][:, 0:1]
            normed = (u_s[i].astype(F32) - mean_s[i][:, 0:1]) * inverse
            first = jnp.mean(grad_normed, axis=-1, keepdims=True)
            second = jnp.mean(grad_normed * normed, axis=-1, keepdims=True)
            mixture = (grad_normed - first - normed * second) * inverse
            gout[i] = (e_g[mine, :].astype(F32) + mixture).astype(BF)

            @pl.when(deep)
            def _():
                remote(gout.at[i], tin.at[i], act_send.at[1, i], act_recv.at[1, i], mirror).start()
                for n, (lo, size) in enumerate(CHUNKS):
                    cols = pl.ds(lo, size)
                    cout[i, :, cols] = dot(gout[i], wt_jn[:, cols]).astype(BF)
                    remote(cout.at[i, :, cols], cin.at[i, :, cols], c_send.at[i, n], c_recv.at[i, n], z_down).start()

            @pl.when(jnp.logical_not(deep))
            def _():
                for n, (lo, size) in enumerate(CHUNKS):
                    cols = pl.ds(lo, size)
                    remote(gout.at[i, :, cols], cin.at[i, :, cols], c_send.at[i, n], c_recv.at[i, n], z_down).start()

        show(2, i)
        show(3, i)

        @pl.when(deep)
        def _():
            right_g[mine, :] = gout[i]

        @pl.when(z > EARLY)
        def _():
            show(5, i)

        return 0

    lax.fori_loop(0, count, backward, 0)

    @pl.when(z > EARLY)
    def _():
        turn_activations()

    seen(2)
    partials(1, active_t, e_g, 288)
    launch(1)
    seen(3)
    partials(0, scaled_t, gp_g, 144)
    launch(0)

    @pl.when(z > EARLY)
    def _():
        join_partials()
        launch(2)

    @pl.when(z == 0)
    def _():
        collect((1, 0))

    @pl.when(z > 0)
    def _():
        collect((1, 0, 2))

    for m in (2, 1, 0):
        await_bytes(outs[m], o_recv.at[m])

    for m in range(3):
        swap_sent(ins[m], swap_send.at[m])
        swap_sent(outs[m], o_send.at[m])
        await_bytes(gs[m].at[pl.ds(0, 135)], rs_send.at[m])
    swap_sent(st_gain, swap_send.at[3])

    def all_sent(i, _):
        for n, (lo, size) in enumerate(CHUNKS):
            part = hout.at[i, :, pl.ds(lo, size)]

            @pl.when(z < 7)
            def _():
                await_bytes(part, h_send.at[i, n])

            @pl.when(z > 0)
            def _():
                await_bytes(part, c_send.at[i, n])

        @pl.when(jnp.logical_not(deep))
        def _():
            await_bytes(skout.at[i], act_send.at[0, i])

        @pl.when(deep)
        def _():
            await_bytes(gout.at[i], act_send.at[1, i])

        for kind in range(6):
            await_bytes(shared[kind].at[rows(first + i)], x_send.at[kind, first + i])
        return 0

    lax.fori_loop(0, count, all_sent, 0)


def widen(up, dn, jn, up_out, dn_out, jn_out):
    up_out[...] = up[...].astype(F32).reshape(up_out.shape)
    dn_out[...] = dn[...].astype(F32).reshape(dn_out.shape)
    jn_out[...] = jn[...].astype(F32).reshape(jn_out.shape)


def vm(*shape, dtype=BF):
    return pltpu.VMEM(shape, dtype)


def local(latents, time_table, timesteps, order, gains, w_up, w_down, w_join, cotangent):
    act = (MICROS, ROWS, D)
    tokens = GROUPS * ROWS
    chunks = len(CHUNKS)
    dma = pltpu.SemaphoreType.DMA
    full = [vm(D, FFW), vm(FFW, D), vm(D, D)]
    scratch = (
        [vm(288, *u) for u in UNIT]
        + full
        + [vm(FFW, D), vm(D, FFW), vm(D, D)]
        + [vm(135, *u) for u in UNIT]
        + [vm(9, *u) for u in UNIT]
        + [vm(8, D, dtype=F32), vm(8, D, dtype=F32)]
        + [vm(*act) for _ in range(9)]
        + [
            vm(MICROS, ROWS, FFW, dtype=F32), vm(MICROS, ROWS, 128, dtype=F32), vm(MICROS, ROWS, 128, dtype=F32),
            vm(*act, dtype=F32), vm(tokens, D), vm(tokens, FFW), vm(tokens, D), vm(tokens, FFW), vm(tokens, D),
            vm(tokens, D), vm(D, tokens), vm(FFW, tokens),
        ]
        + [
            dma, dma((4,)), dma((4,)), dma((2, 4, chunks)), dma((3, 2, 16)), dma((3,)), dma((3,)), dma((3,)),
            dma((MICROS, chunks)), dma((MICROS, chunks)), dma((MICROS, chunks)), dma((MICROS, chunks)),
            dma((2, MICROS)), dma((2, MICROS)), dma((6, GROUPS)), dma((6, GROUPS)),
            dma((3, 2, 15)), dma((3,)), dma((3,)), dma((3,)),
        ]
    )
    spec = pl.BlockSpec(memory_space=pltpu.VMEM)
    sums = pl.pallas_call(
        kernel,
        out_shape=[jax.ShapeDtypeStruct((9,) + u, BF) for u in UNIT],
        in_specs=[pl.BlockSpec(memory_space=pltpu.SMEM)] * 2 + [spec] * 5 + [pl.BlockSpec(memory_space=pl.ANY), spec],
        out_specs=[spec] * 3,
        scratch_shapes=scratch,
        compiler_params=pltpu.CompilerParams(
            collective_id=0, has_side_effects=True, vmem_limit_bytes=63 * 2**20
        ),
        name="blocks",
    )(timesteps, order, w_up[0], w_down[0], w_join[0], gains, latents, time_table.reshape(-1, 8, D), cotangent.reshape(4, ROWS, D))
    up, down, join = pl.pallas_call(
        widen,
        out_shape=[
            jax.ShapeDtypeStruct((36, 1, FFW), F32),
            jax.ShapeDtypeStruct((72, D), F32),
            jax.ShapeDtypeStruct((36, 1, D), F32),
        ],
        in_specs=[spec] * 3,
        out_specs=[spec] * 3,
        name="widen",
    )(*sums)
    return jnp.swapaxes(up, 0, 1), down[None], jnp.swapaxes(join, 0, 1)


def solution(mesh):
    in_specs = (
        P(None, "dp", None),
        P(),
        P(),
        P(),
        P("section", None),
        P("section", "dp", None),
        P("section", "dp", None),
        P("section", "dp", None),
        P(None, "dp", None),
    )
    out_specs = (P("section", "dp", None), P("section", "dp", None), P("section", "dp", None))
    return jax.shard_map(local, mesh=mesh, in_specs=in_specs, out_specs=out_specs, check_vma=False)
```

time: 212 us -> 201 us (0.948)
  Pallas kernels: 208 us -> 197 us
    pallas_call x1, Pallas kernels: 203 us -> 195 us  [local(): pl.pallas_call(kernel, out_shape=[jax.ShapeDtypeStruct((9,) + u, BF) for...]
    pallas_call x1 -> x0, Pallas kernels: 2.42 us -> none  [local(): pl.pallas_call(pick, grid_spec=pltpu.PrefetchScalarGridSpec(num_scalar_pr...]
where the time goes in v3:
time: 201 us; the launch traced here: 197 us
  Pallas kernels  197 us (98%)
    pallas_call x1, Pallas kernels, local(): pl.pallas_call(kernel, out_shape=[jax.ShapeDtypeStruct((9,) + u, BF) for...  195 us

profile of v3, /device:TPU:32, one launch (start us, length us, event | category | flops | bytes accessed | tf_op | source)
XLA Modules:
  0.0 197.4 jit_solution(7427007251502030038)
XLA Ops:
  0.6 194.8 %blocks.1 = (bf16[9,4,2304]{2,1,0:T(4,128)(2,1)}, bf16[9,8,1152]{2,1,0:T(8,128)(2,1)}, bf16[9,4,1152]{2,1,0:T(4,128)(2,1)}) custom-call(s32[2]{0:T(128)} %steps.1, s32[2]{0:T(128)} %order.1, bf16[36,2304]{1,0:T(8,128)(2,1)} %bitcast.10, bf16[72,1152]{1,0:T(8,128)(2,1)} %bitcast.11, bf16[36,1152]{1,0:T(8,128)(2,1)} %bitcast.12, bf16[1,1152]{1,0:T(2,128)(2,1)} %gain_in.1, ...), custom_call_target="tpu_custom_call" | custom-call | tf_op jit(solution)/shard_map/blocks/pallas_call | solution.py:643
  195.5 2.0 widen.1

commit v4 on v3

--- a/solution.py
+++ b/solution.py
@@ -14,7 +14,7 @@
 ROWS = 32
 GROUPS = 8
 FEWER, MICROS = 3, 5
-EARLY = 2
+EARLY = 1
 CHUNKS = ((0, 512), (512, 640))
 PART = (((0, 5, 1), (5, 4, -1)), ((0, 4, -1), (4, 5, 1)), ((0, 4, 1), (4, 5, -1)))
 UNIT = ((4, FFW), (8, D), (4, D))
@@ -45,7 +45,7 @@
     st_up, st_dn, st_jn, st_gain, gain, hin, skin, cin, tin, u_s, hout, skout, cout, gout,
     dg_s, mean_s, inv_s, turned_s, scaled_g, active_g, e_g, gp_g, left_g, right_g, scaled_t, active_t,
     time_sem, swap_sem, swap_send, io_send, ag_recv, ag_send, f_recv, f_send,
-    h_recv, h_send, c_recv, c_send, act_recv, act_send, x_recv, x_send, rs_recv, rs_send, o_recv, o_send,
+    h_recv, h_send, c_recv, c_send, act_recv, act_send, x_recv, x_send, rs_recv, rs_send, o_send,
 ):
     q = lax.axis_index("dp")
     s = lax.axis_index("section")
@@ -66,10 +66,13 @@
     swap = device(x, y, 2 * zh + c, zl)
     stays = zl == c
 
-    def along(axis, step):
+    def along(axis, step, plane=z, core=c):
         if axis == 0:
-            return device(rem(x + 4 + step, 4), y, z, c)
-        return device(x, rem(y + 4 + step, 4), z, c)
+            return device(rem(x + 4 + step, 4), y, plane, core)
+        return device(x, rem(y + 4 + step, 4), plane, core)
+
+    def holder_along(axis, step):
+        return along(axis, step, 2 * zh + c, zl)
 
     other = device(x, y, 2 * zh + 1 - zl, 1 - c)
 
@@ -111,6 +114,7 @@
 
     barrier = pltpu.get_barrier_semaphore()
     greet = [along(0, 1), along(0, -1), along(1, 1), along(1, -1), partner, z_up, z_down, mirror, other]
+    greet += [holder_along(0, 1), holder_along(0, -1), holder_along(1, 1), holder_along(1, -1)]
     for peer in greet:
         pl.semaphore_signal(barrier, inc=1, device_id=peer, device_id_type=MESH)
     pl.semaphore_wait(barrier, len(greet))
@@ -332,7 +336,7 @@
 
         @pl.when(jnp.logical_not(deep))
         def _():
-            @pl.when(z > EARLY)
+            @pl.when(z > 2)
             def _():
                 give_skip(i)
 
@@ -341,6 +345,67 @@
         show(0, i)
         show(1, i)
         show(4, i)
+        return 0
+
+    def backward(i, _):
+        mine = rows(first + i)
+
+        @pl.when(deep)
+        def _():
+            for n, (lo, size) in enumerate(CHUNKS):
+                await_bytes(cin.at[i, :, pl.ds(lo, size)], c_recv.at[i, n])
+            e_g[mine, :] = cin[i]
+
+        @pl.when(jnp.logical_not(deep))
+        def _():
+            @pl.when(z > EARLY)
+            def _():
+                await_bytes(tin.at[i], act_recv.at[1, i])
+                right_g[mine, :] = tin[i]
+                turned_s[i] = dot(tin[i], wt_jn[...])
+
+            for n, (lo, size) in enumerate(CHUNKS):
+                await_bytes(cin.at[i, :, pl.ds(lo, size)], c_recv.at[i, n])
+            e_g[mine, :] = (cin[i].astype(F32) + turned_s[i]).astype(BF)
+
+        back_in = dot(e_g[mine, :], wt_dn[...])
+        gp_g[mine, :] = (dg_s[i] * back_in).astype(BF)
+
+        @pl.when(z > 0)
+        def _():
+            grad_normed = dot(gp_g[mine, :], wt_up[...]) * gain[0:1, :]
+            inverse = inv_s[i][:, 0:1]
+            normed = (u_s[i].astype(F32) - mean_s[i][:, 0:1]) * inverse
+            first = jnp.mean(grad_normed, axis=-1, keepdims=True)
+            second = jnp.mean(grad_normed * normed, axis=-1, keepdims=True)
+            mixture = (grad_normed - first - normed * second) * inverse
+            gout[i] = (e_g[mine, :].astype(F32) + mixture).astype(BF)
+
+            @pl.when(deep)
+            def _():
+                remote(gout.at[i], tin.at[i], act_send.at[1, i], act_recv.at[1, i], mirror).start()
+                for n, (lo, size) in enumerate(CHUNKS):
+                    cols = pl.ds(lo, size)
+                    cout[i, :, cols] = dot(gout[i], wt_jn[:, cols]).astype(BF)
+                    remote(cout.at[i, :, cols], cin.at[i, :, cols], c_send.at[i, n], c_recv.at[i, n], z_down).start()
+
+            @pl.when(jnp.logical_not(deep))
+            def _():
+                for n, (lo, size) in enumerate(CHUNKS):
+                    cols = pl.ds(lo, size)
+                    remote(gout.at[i, :, cols], cin.at[i, :, cols], c_send.at[i, n], c_recv.at[i, n], z_down).start()
+
+        show(2, i)
+        show(3, i)
+
+        @pl.when(deep)
+        def _():
+            right_g[mine, :] = gout[i]
+
+        @pl.when(z > EARLY)
+        def _():
+            show(5, i)
+
         return 0
 
     for i in range(4):
@@ -365,13 +430,23 @@
     def _():
         transposes()
 
-    lax.fori_loop(0, count, forward, 0)
+    @pl.when(z < 7)
+    def _():
+        lax.fori_loop(0, count, forward, 0)
+
+    @pl.when(z == 7)
+    def _():
+        def both(i, _):
+            forward(i, 0)
+            return backward(i, 0)
+
+        lax.fori_loop(0, count, both, 0)
 
     @pl.when(z <= 1)
     def _():
         gather((2,))
 
-    @pl.when(z <= EARLY)
+    @pl.when(z <= 2)
     def _():
         def one(i, _):
             give_skip(i)
@@ -415,19 +490,18 @@
 
     def landing(m, h, n):
         cnt = PART[m][h][1]
-        return pl.ds((0 if h == 0 else 15 * PART[m][0][1]) + n * cnt, cnt)
-
-    def pass_on(m, h, mine, axis, step, n):
-        remote(
-            gs[m].at[mine], rrs[m].at[landing(m, h, n)], rs_send.at[m], rs_recv.at[m, h, n], along(axis, step)
-        ).start()
+        return pl.ds((0 if h == 0 else 16 * PART[m][0][1]) + n * cnt, cnt)
+
+    def pass_on(m, h, mine, dev, n):
+        remote(gs[m].at[mine], rrs[m].at[landing(m, h, n)], rs_send.at[m], rs_recv.at[m, h, n], dev).start()
 
     def launch(m):
-        def one(i, _):
+        def one(t, _):
+            i = rem(t + 2, 4)
             for h in range(2):
                 d = PART[m][h][2]
-                pass_on(m, h, piece_rows(m, h, i, 2), h, -d, i)
-                pass_on(m, h, piece_rows(m, h, i, 3), h, d, 4 + i)
+                pass_on(m, h, piece_rows(m, h, i, 2), along(h, -d), i)
+                pass_on(m, h, piece_rows(m, h, i, 3), along(h, d), 4 + i)
             return 0
 
         lax.fori_loop(0, 4, one, 0)
@@ -445,22 +519,22 @@
             gs[m][mine] = total.astype(BF)
             return mine
 
-        def middle(i, _):
+        def middle(t, _):
+            i = rem(t + 2, 4)
             for m, h in parts:
-                pass_on(m, h, settle(m, h, i, 1, (i,)), h, -PART[m][h][2], 8 + i)
+                pass_on(m, h, settle(m, h, i, 1, (i,)), along(h, -PART[m][h][2]), 8 + i)
             return 0
 
         lax.fori_loop(0, 4, middle, 0)
         for m, h in parts:
-            pass_on(m, h, settle(m, h, 2, 0, (6, 10)), 1 - h, -PART[m][h][2], 12)
+            pass_on(m, h, settle(m, h, 2, 0, (6, 10)), along(1 - h, -PART[m][h][2]), 12)
         for m, h in parts:
-            pass_on(m, h, settle(m, h, 3, 0, (7, 11)), 1 - h, PART[m][h][2], 14)
+            pass_on(m, h, settle(m, h, 3, 0, (7, 11)), holder_along(1 - h, PART[m][h][2]), 14)
         for m, h in parts:
-            pass_on(m, h, settle(m, h, 1, 0, (5, 9, 12)), 1 - h, -PART[m][h][2], 13)
+            mine = settle(m, h, 0, 0, (4, 8))
+            swap_copy(gs[m].at[mine], rrs[m].at[landing(m, h, 15)], o_send.at[m, h], rs_recv.at[m, h, 15])
         for m, h in parts:
-            settle(m, h, 0, 0, (4, 8, 13, 14))
-            if h == 1:
-                swap_copy(gs[m].at[pl.ds(9 * own, 9)], outs[m], o_send.at[m], o_recv.at[m])
+            pass_on(m, h, settle(m, h, 1, 0, (5, 9, 12)), holder_along(1 - h, -PART[m][h][2]), 13)
 
     @pl.when(z <= EARLY)
     def _():
@@ -476,72 +550,13 @@
         launch(2)
         turn_activations()
 
-    @pl.when(z == 0)
+    @pl.when(z <= EARLY)
     def _():
         collect((2,))
 
-    def backward(i, _):
-        mine = rows(first + i)
-
-        @pl.when(deep)
-        def _():
-            for n, (lo, size) in enumerate(CHUNKS):
-                await_bytes(cin.at[i, :, pl.ds(lo, size)], c_recv.at[i, n])
-            e_g[mine, :] = cin[i]
-
-        @pl.when(jnp.logical_not(deep))
-        def _():
-            @pl.when(z > EARLY)
-            def _():
-                await_bytes(tin.at[i], act_recv.at[1, i])
-                right_g[mine, :] = tin[i]
-                turned_s[i] = dot(tin[i], wt_jn[...])
-
-            for n, (lo, size) in enumerate(CHUNKS):
-                await_bytes(cin.at[i, :, pl.ds(lo, size)], c_recv.at[i, n])
-            e_g[mine, :] = (cin[i].astype(F32) + turned_s[i]).astype(BF)
-
-        back_in = dot(e_g[mine, :], wt_dn[...])
-        gp_g[mine, :] = (dg_s[i] * back_in).astype(BF)
-
-        @pl.when(z > 0)
-        def _():
-            grad_normed = dot(gp_g[mine, :], wt_up[...]) * gain[0:1, :]
-            inverse = inv_s[i][:, 0:1]
-            normed = (u_s[i].astype(F32) - mean_s[i][:, 0:1]) * inverse
-            first = jnp.mean(grad_normed, axis=-1, keepdims=True)
-            second = jnp.mean(grad_normed * normed, axis=-1, keepdims=True)
-            mixture = (grad_normed - first - normed * second) * inverse
-            gout[i] = (e_g[mine, :].astype(F32) + mixture).astype(BF)
-
-            @pl.when(deep)
-            def _():
-                remote(gout.at[i], tin.at[i], act_send.at[1, i], act_recv.at[1, i], mirror).start()
-                for n, (lo, size) in enumerate(CHUNKS):
-                    cols = pl.ds(lo, size)
-                    cout[i, :, cols] = dot(gout[i], wt_jn[:, cols]).astype(BF)
-                    remote(cout.at[i, :, cols], cin.at[i, :, cols], c_send.at[i, n], c_recv.at[i, n], z_down).start()
-
-            @pl.when(jnp.logical_not(deep))
-            def _():
-                for n, (lo, size) in enumerate(CHUNKS):
-                    cols = pl.ds(lo, size)
-                    remote(gout.at[i, :, cols], cin.at[i, :, cols], c_send.at[i, n], c_recv.at[i, n], z_down).start()
-
-        show(2, i)
-        show(3, i)
-
-        @pl.when(deep)
-        def _():
-            right_g[mine, :] = gout[i]
-
-        @pl.when(z > EARLY)
-        def _():
-            show(5, i)
-
-        return 0
-
-    lax.fori_loop(0, count, backward, 0)
+    @pl.when(z < 7)
+    def _():
+        lax.fori_loop(0, count, backward, 0)
 
     @pl.when(z > EARLY)
     def _():
@@ -559,20 +574,28 @@
         join_partials()
         launch(2)
 
-    @pl.when(z == 0)
+    @pl.when(z <= EARLY)
     def _():
         collect((1, 0))
 
-    @pl.when(z > 0)
+    @pl.when(z > EARLY)
     def _():
         collect((1, 0, 2))
 
     for m in (2, 1, 0):
-        await_bytes(outs[m], o_recv.at[m])
+        for h in range(2):
+            off, cnt, _ = PART[m][h]
+            total = 0.0
+            for n in (14, 15, 13):
+                spot = landing(m, h, n)
+                await_bytes(rrs[m].at[spot], rs_recv.at[m, h, n])
+                total = total + rrs[m][spot].astype(F32)
+            outs[m][off:off + cnt] = total.astype(BF)
 
     for m in range(3):
         swap_sent(ins[m], swap_send.at[m])
-        swap_sent(outs[m], o_send.at[m])
+        for h in range(2):
+            swap_sent(rrs[m].at[landing(m, h, 15)], o_send.at[m, h])
         await_bytes(gs[m].at[pl.ds(0, 135)], rs_send.at[m])
     swap_sent(st_gain, swap_send.at[3])
 
@@ -623,7 +646,7 @@
         [vm(288, *u) for u in UNIT]
         + full
         + [vm(FFW, D), vm(D, FFW), vm(D, D)]
-        + [vm(135, *u) for u in UNIT]
+        + [vm(144, *u) for u in UNIT]
         + [vm(9, *u) for u in UNIT]
         + [vm(8, D, dtype=F32), vm(8, D, dtype=F32)]
         + [vm(*act) for _ in range(9)]
@@ -636,7 +659,7 @@
             dma, dma((4,)), dma((4,)), dma((2, 4, chunks)), dma((3, 2, 16)), dma((3,)), dma((3,)), dma((3,)),
             dma((MICROS, chunks)), dma((MICROS, chunks)), dma((MICROS, chunks)), dma((MICROS, chunks)),
             dma((2, MICROS)), dma((2, MICROS)), dma((6, GROUPS)), dma((6, GROUPS)),
-            dma((3, 2, 15)), dma((3,)), dma((3,)), dma((3,)),
+            dma((3, 2, 16)), dma((3,)), dma((3, 2)),
         ]
     )
     spec = pl.BlockSpec(memory_space=pltpu.VMEM)

time: 201 us -> 190 us (0.945); the launches traced: 197 us -> 189 us
  Pallas kernels: 197 us -> 189 us
    pallas_call x1, Pallas kernels: 195 us -> 187 us  [local(): pl.pallas_call(kernel, out_shape=[jax.ShapeDtypeStruct((9,) + u, BF) for...]
where the time goes in v4:
time: 190 us; the launch traced here: 189 us
  Pallas kernels  189 us (99%)
    pallas_call x1, Pallas kernels, local(): pl.pallas_call(kernel, out_shape=[jax.ShapeDtypeStruct((9,) + u, BF) for...  187 us

profile of v4, /device:TPU:32, one launch (start us, length us, event | category | flops | bytes accessed | tf_op | source)
XLA Modules:
  0.0 189.4 jit_solution(11189275540565046094)
XLA Ops:
  0.6 186.8 %blocks.1 = (bf16[9,4,2304]{2,1,0:T(4,128)(2,1)}, bf16[9,8,1152]{2,1,0:T(8,128)(2,1)}, bf16[9,4,1152]{2,1,0:T(4,128)(2,1)}) custom-call(s32[2]{0:T(128)} %steps.1, s32[2]{0:T(128)} %order.1, bf16[36,2304]{1,0:T(8,128)(2,1)} %bitcast.10, bf16[72,1152]{1,0:T(8,128)(2,1)} %bitcast.11, bf16[36,1152]{1,0:T(8,128)(2,1)} %bitcast.12, bf16[1,1152]{1,0:T(2,128)(2,1)} %gain_in.1, ...), custom_call_target="tpu_custom_call" | custom-call | tf_op jit(solution)/shard_map/blocks/pallas_call | solution.py:666
  187.5 2.0 %widen.1 = (f32[36,1,2304]{2,1,0:T(1,128)}, f32[72,1152]{1,0:T(8,128)}, f32[36,1,1152]{2,1,0:T(1,128)}) custom-call(bf16[9,4,2304]{2,1,0:T(4,128)(2,1)} %get-tuple-element.9.up, bf16[9,8,1152]{2,1,0:T(8,128)(2,1)} %get-tuple-element.10.dn, bf16[9,4,1152]{2,1,0:T(4,128)(2,1)} %get-tuple-element.11.jn), custom_call_target="tpu_custom_call" | custom-call | tf_op jit(solution)/shard_map/widen/pallas_call | solution.py:677

commit v5 on v4

--- a/solution.py
+++ b/solution.py
@@ -106,17 +106,18 @@
         def _():
             await_bytes(src, send)
 
+    barrier = pltpu.get_barrier_semaphore()
+    greet = [along(0, 1), along(0, -1), along(1, 1), along(1, -1), partner, z_up, z_down, mirror, other]
+    greet += [holder_along(0, 1), holder_along(0, -1), holder_along(1, 1), holder_along(1, -1)]
+    for peer in greet:
+        pl.semaphore_signal(barrier, inc=1, device_id=peer, device_id_type=MESH)
+
     ins = (st_up, st_dn, st_jn)
     st_up[...] = up_in[...].reshape((9,) + UNIT[0])
     st_dn[...] = dn_in[...].reshape((9,) + UNIT[1])
     st_jn[...] = jn_in[...].reshape((9,) + UNIT[2])
     st_gain[...] = jnp.broadcast_to(gain_in[...].astype(F32), (8, D))
 
-    barrier = pltpu.get_barrier_semaphore()
-    greet = [along(0, 1), along(0, -1), along(1, 1), along(1, -1), partner, z_up, z_down, mirror, other]
-    greet += [holder_along(0, 1), holder_along(0, -1), holder_along(1, 1), holder_along(1, -1)]
-    for peer in greet:
-        pl.semaphore_signal(barrier, inc=1, device_id=peer, device_id_type=MESH)
     pl.semaphore_wait(barrier, len(greet))
 
     for m in range(3):
@@ -462,15 +463,6 @@
         await_bytes(gs[m].at[pl.ds(0, 135)], ag_send.at[m])
         await_bytes(gs[m].at[pl.ds(0, 144)], f_send.at[m])
 
-    def partials(m, left, right, size):
-        def one(j, _):
-            t = 2 * j + c
-            part = dot(left[pl.ds(pl.multiple_of(t * size, size), size), :], right[...])
-            gs[m][pl.ds(36 * t, 36)] = part.reshape((36,) + UNIT[m]).astype(BF)
-            return 0
-
-        lax.fori_loop(0, 4, one, 0)
-
     def turn_activations():
         seen(0)
         seen(1)
@@ -495,13 +487,31 @@
     def pass_on(m, h, mine, dev, n):
         remote(gs[m].at[mine], rrs[m].at[landing(m, h, n)], rs_send.at[m], rs_recv.at[m, h, n], dev).start()
 
-    def launch(m):
-        def one(t, _):
-            i = rem(t + 2, 4)
-            for h in range(2):
-                d = PART[m][h][2]
-                pass_on(m, h, piece_rows(m, h, i, 2), along(h, -d), i)
-                pass_on(m, h, piece_rows(m, h, i, 3), along(h, d), 4 + i)
+    def partials(m, left, right, size):
+        def far(h, i):
+            pass_on(m, h, piece_rows(m, h, i, 2), along(h, -PART[m][h][2]), i)
+
+        def near(h, i):
+            pass_on(m, h, piece_rows(m, h, i, 3), along(h, PART[m][h][2]), 4 + i)
+
+        def one(step, _):
+            t = 2 * rem(x + 2 + step, 4) + c
+            part = dot(left[pl.ds(pl.multiple_of(t * size, size), size), :], right[...])
+            gs[m][pl.ds(36 * t, 36)] = part.reshape((36,) + UNIT[m]).astype(BF)
+            i = rem(16 - PART[m][1][2] * (step + 2), 4)
+            far(1, i)
+            near(1, i)
+
+            @pl.when(step == 0)
+            def _():
+                for i in (2, 3, 0, 1):
+                    far(0, i)
+
+            @pl.when(step == 2 + PART[m][0][2])
+            def _():
+                for i in (2, 3, 0, 1):
+                    near(0, i)
+
             return 0
 
         lax.fori_loop(0, 4, one, 0)
@@ -547,7 +557,6 @@
 
         lax.fori_loop(0, count, one, 0)
         join_partials()
-        launch(2)
         turn_activations()
 
     @pl.when(z <= EARLY)
@@ -564,15 +573,12 @@
 
     seen(2)
     partials(1, active_t, e_g, 288)
-    launch(1)
     seen(3)
     partials(0, scaled_t, gp_g, 144)
-    launch(0)
 
     @pl.when(z > EARLY)
     def _():
         join_partials()
-        launch(2)
 
     @pl.when(z <= EARLY)
     def _():

time: 190 us -> 189 us (level)
  no operation moved by 1% of the time
where the time goes in v5:
time: 189 us
  Pallas kernels  188 us (99%)
    pallas_call x1, Pallas kernels, local(): pl.pallas_call(kernel, out_shape=[jax.ShapeDtypeStruct((9,) + u, BF) for...  186 us

profile of v5, /device:TPU:32, one launch (start us, length us, event | category | flops | bytes accessed | tf_op | source)
XLA Modules:
  0.0 188.8 jit_solution(15159381970478554513)
XLA Ops:
  0.6 186.2 %blocks.1 = (bf16[9,4,2304]{2,1,0:T(4,128)(2,1)}, bf16[9,8,1152]{2,1,0:T(8,128)(2,1)}, bf16[9,4,1152]{2,1,0:T(4,128)(2,1)}) custom-call(s32[2]{0:T(128)} %steps.1, s32[2]{0:T(128)} %order.1, bf16[36,2304]{1,0:T(8,128)(2,1)} %bitcast.10, bf16[72,1152]{1,0:T(8,128)(2,1)} %bitcast.11, bf16[36,1152]{1,0:T(8,128)(2,1)} %bitcast.12, bf16[1,1152]{1,0:T(2,128)(2,1)} %gain_in.1, ...), custom_call_target="tpu_custom_call" | custom-call | tf_op jit(solution)/shard_map/blocks/pallas_call | solution.py:672
  186.8 2.0 %widen.1 = (f32[36,1,2304]{2,1,0:T(1,128)}, f32[72,1152]{1,0:T(8,128)}, f32[36,1,1152]{2,1,0:T(1,128)}) custom-call(bf16[9,4,2304]{2,1,0:T(4,128)(2,1)} %get-tuple-element.9.up, bf16[9,8,1152]{2,1,0:T(8,128)(2,1)} %get-tuple-element.10.dn, bf16[9,4,1152]{2,1,0:T(4,128)(2,1)} %get-tuple-element.11.jn), custom_call_target="tpu_custom_call" | custom-call | tf_op jit(solution)/shard_map/widen/pallas_call | solution.py:683
